TPU v7x, 256 devices: a whole 4x4x8 slice. The times are simulated.
256 devices in a mesh: seq: 64 (over z, y, core), mp: 4 (over x).
Axes of the slice: x: 4, y: 4, z: 8, core: 2. Of those that a mesh axis runs over, the one named last changes fastest.
Arguments:
- tokens: bfloat16 [1, 16384, 768], P(None, 'seq'), may hold values from -16 to 16
- w_qkv: bfloat16 [3, 768, 768], P(None, 'mp'), may hold values from -0.21875 to 0.21875
- w_out: bfloat16 [768, 768], P('mp'), may hold values from -0.21875 to 0.21875
- grad_y: bfloat16 [1, 16384, 768], P(None, 'seq'), may hold values from -16 to 16
Outputs:
- mixed: bfloat16 [1, 16384, 768], P(None, 'seq', 'mp')
- grad_tokens: bfloat16 [1, 16384, 768], P(None, 'seq', 'mp')
- grad_wqkv: float32 [768, 3, 768], P('seq', None, 'mp')
- grad_wout: float32 [768, 768], P('seq', 'mp')
All inputs are finite; a program needn't handle non-finite values.
Results may differ from a plain program's by a relative error of at most 0.029.
Values may be sent and summed in bfloat16 or wider, within the bound.
A program may use at most 64 MiB of HBM per device.

v0:
```python
import math

import jax
import jax.numpy as jnp
from jax import lax
from jax.sharding import PartitionSpec as P

HEAD = 64
BLOCK = 128
LEVELS = 4


SCORE_SCALE = 32.0
NORM_EPSILON = 1e-06
ROOT_HALF = 0.7071067811865476
FAR_OFFSETS = (-3, -2, 2, 3)
EVEN_KEEP = (0.0, 1.0, 1.0, 1.0)
ODD_KEEP = (1.0, 1.0, 1.0, 0.0)


def as_sent(shard):

    def short(part):
        return part.astype(jnp.bfloat16) if part.dtype == jnp.float32 else part

    return jax.tree.map(short, shard)


def swapped(shard, axis, bit):
    return lax.ppermute(shard, axis, [(i, i ^ 1 << bit) for i in range(lax.axis_size(axis))])


def shifted(value, axis, steps):
    count = lax.axis_size(axis)
    leading, last = (max(0, -steps), min(count, count - steps))
    return lax.ppermute(value, axis, [(source, source + steps) for source in range(leading, last)])


def with_halo(block, sides, width):
    for axis, dim in sides:
        count = lax.axis_size(axis)
        forward = [(i, i + 1) for i in range(count - 1)]
        backward = [(target, source) for source, target in forward]
        low = lax.ppermute(
            lax.slice_in_dim(block, block.shape[dim] - width, None, axis=dim), axis, forward
        )
        high = lax.ppermute(lax.slice_in_dim(block, 0, width, axis=dim), axis, backward)
        block = jnp.concatenate([low, block, high], axis=dim)
    return block


def unit_rows(vector):
    return vector * lax.rsqrt(jnp.mean(vector * vector, axis=-1, keepdims=True) + NORM_EPSILON)


def pair_rows(vector):
    extent = vector.shape
    return vector.reshape(extent[0], extent[1] // 2, 2, extent[2], extent[3])


def pyramid(query_pre, key_pre, value_pre):
    query_float = unit_rows(query_pre)
    key_float = unit_rows(key_pre)
    value_float = value_pre
    levels_out = []
    for level_index in range(LEVELS):
        if level_index > 0:
            query_float = unit_rows(jnp.mean(pair_rows(query_float), axis=2))
            key_float = unit_rows(jnp.mean(pair_rows(key_float), axis=2))
            value_float = jnp.sum(pair_rows(value_float), axis=2) * ROOT_HALF
        levels_out.append(
            (
                query_float.astype(jnp.bfloat16),
                key_float.astype(jnp.bfloat16),
                value_float.astype(jnp.bfloat16),
            )
        )
    return tuple(levels_out)


def pool_total(values_in, factor):
    extent = values_in.shape
    return jnp.sum(values_in.reshape((extent[0], extent[1] // factor, factor) + extent[2:]), axis=2)


def merge_heads(values_in):
    extent = values_in.shape
    return values_in.reshape(extent[:-2] + (extent[-2] * extent[-1],))


def joined(key_part, value_part):
    return jnp.concatenate([merge_heads(key_part), merge_heads(value_part)], axis=-1)


def split_heads(packed_rows, features, local_heads, part_index):
    chosen = packed_rows[..., part_index * features : (part_index + 1) * features]
    return chosen.reshape(chosen.shape[:-1] + (local_heads, HEAD))


def near_keep(where_seq, seq_devices):
    first_ok = (where_seq > 0).astype(jnp.float32)
    last_ok = (where_seq < seq_devices - 1).astype(jnp.float32)
    one_value = jnp.ones((), jnp.float32)
    row_keep = jnp.stack([first_ok, first_ok, one_value, one_value, last_ok, last_ok])
    return jnp.stack([row_keep, row_keep])


def far_keep(where_seq, seq_devices, group_size):
    block_id = where_seq // group_size
    block_total = seq_devices // group_size
    moved = block_id + jnp.array(FAR_OFFSETS, jnp.int32)
    exists = ((moved >= 0) & (moved < block_total)).astype(jnp.float32)
    parity = jnp.where(
        block_id % 2 == 0, jnp.array(EVEN_KEEP, jnp.float32), jnp.array(ODD_KEEP, jnp.float32)
    )
    return (exists * parity)[None, :]


def block_weights(query_blocks, key_blocks, keep_mask, scale_level):
    scores = jnp.einsum(
        "sqihe,sqjhe->sqhij", query_blocks, key_blocks, preferred_element_type=jnp.float32
    ) * (SCORE_SCALE / HEAD)
    column_keep = jnp.repeat(keep_mask, BLOCK, axis=1)
    return jnp.exp(scores) * (scale_level * column_keep[None, :, None, None, :])


def block_forward(query_blocks, key_blocks, value_blocks, keep_mask, scale_level):
    weights = block_weights(query_blocks, key_blocks, keep_mask, scale_level)
    numer_part = jnp.einsum(
        "sqhij,sqjhe->sqihe",
        weights.astype(jnp.bfloat16),
        value_blocks,
        preferred_element_type=jnp.float32,
    )
    denom_part = jnp.swapaxes(jnp.sum(weights, axis=-1), 2, 3)
    return (numer_part, denom_part)


def block_backward(
    query_blocks, key_blocks, value_blocks, keep_mask, scale_level, pulled, offset_sum
):
    weights = block_weights(query_blocks, key_blocks, keep_mask, scale_level)
    pulled_low = pulled.astype(jnp.bfloat16)
    inner_dots = jnp.einsum(
        "sqihe,sqjhe->sqhij", pulled_low, value_blocks, preferred_element_type=jnp.float32
    )
    centred = jnp.swapaxes(offset_sum, 2, 3)[..., None]
    slopes = (weights * (inner_dots - centred) * (SCORE_SCALE / HEAD)).astype(jnp.bfloat16)
    d_query = jnp.einsum(
        "sqhij,sqjhe->sqihe", slopes, key_blocks, preferred_element_type=jnp.float32
    )
    d_key = jnp.einsum(
        "sqhij,sqihe->sqjhe", slopes, query_blocks, preferred_element_type=jnp.float32
    )
    d_value = jnp.einsum(
        "sqhij,sqihe->sqjhe",
        weights.astype(jnp.bfloat16),
        pulled_low,
        preferred_element_type=jnp.float32,
    )
    return (d_query, d_key, d_value)


def assemble(parts_in, group_size, join_dim, where_seq):
    for bit_index in range(group_size.bit_length() - 1):
        partner = swapped(as_sent(parts_in), "seq", bit_index).astype(parts_in.dtype)
        lower = where_seq // 2**bit_index % 2 == 0
        parts_in = jnp.where(
            lower,
            jnp.concatenate([parts_in, partner], axis=join_dim),
            jnp.concatenate([partner, parts_in], axis=join_dim),
        )
    return parts_in


def split_sum(parts_in, group_size, join_dim, where_seq):
    for bit_index in reversed(range(group_size.bit_length() - 1)):
        half_rows = parts_in.shape[join_dim] // 2
        first_half = lax.slice_in_dim(parts_in, 0, half_rows, axis=join_dim)
        second_half = lax.slice_in_dim(parts_in, half_rows, 2 * half_rows, axis=join_dim)
        lower = where_seq // 2**bit_index % 2 == 0
        kept_half = jnp.where(lower, first_half, second_half)
        sent_half = jnp.where(lower, second_half, first_half)
        parts_in = kept_half + swapped(sent_half.astype(jnp.bfloat16), "seq", bit_index).astype(
            sent_half.dtype
        )
    return parts_in


def fetch_far(rows_in, moved_by):
    return shifted(as_sent(rows_in), "seq", moved_by).astype(rows_in.dtype)


def send_back(rows_in, moved_by):
    return shifted(rows_in.astype(jnp.bfloat16), "seq", moved_by).astype(rows_in.dtype)


def head_total(terms):
    return lax.psum_scatter(
        terms.astype(jnp.bfloat16), "mp", scatter_dimension=2, tiled=True
    ).astype(jnp.float32)


def shards(tokens, w_qkv, w_out, grad_y):
    seq_count, row_count, model_width = tokens.shape
    features = w_qkv.shape[1]
    local_heads = features // HEAD
    seq_devices = lax.axis_size("seq")
    where_seq = lax.axis_index("seq")
    flat_tokens = tokens.reshape(seq_count * row_count, model_width)
    projected = jnp.einsum("td,kcd->tkc", flat_tokens, w_qkv, preferred_element_type=jnp.float32)
    projected = projected.reshape(seq_count, row_count, 3, local_heads, HEAD)
    levels_out, pull_back = jax.vjp(
        pyramid, projected[:, :, 0], projected[:, :, 1], projected[:, :, 2]
    )
    near_query, near_key, near_value = levels_out[0]
    padded = with_halo(as_sent(joined(near_key, near_value)), (("seq", 1),), row_count)
    near_pairs = jnp.stack([padded, padded], axis=1)
    near_keys = split_heads(near_pairs, features, local_heads, 0)
    near_values = split_heads(near_pairs, features, local_heads, 1)
    near_queries = near_query.reshape(seq_count, 2, BLOCK, local_heads, HEAD)
    near_mask = near_keep(where_seq, seq_devices)
    numer_part, denom_part = block_forward(near_queries, near_keys, near_values, near_mask, 1.0)
    numer = numer_part.reshape(seq_count, row_count, local_heads, HEAD)
    denom = denom_part.reshape(seq_count, row_count, local_heads)
    far_saved = []
    for level_index in range(1, LEVELS):
        group_size = 2 ** (level_index - 1)
        query_rows, key_rows, value_rows = levels_out[level_index]
        own_pairs = joined(key_rows, value_rows)
        whole_block = assemble(own_pairs, group_size, 1, where_seq)
        remote = jnp.stack(
            [fetch_far(whole_block, -offset * group_size) for offset in FAR_OFFSETS], axis=1
        )
        remote = remote.reshape(seq_count, 1, len(FAR_OFFSETS) * BLOCK, 2 * features)
        far_keys = split_heads(remote, features, local_heads, 0)
        far_values = split_heads(remote, features, local_heads, 1)
        far_queries = query_rows.reshape(seq_count, 1, query_rows.shape[1], local_heads, HEAD)
        far_mask = far_keep(where_seq, seq_devices, group_size)
        numer_part, denom_part = block_forward(
            far_queries, far_keys, far_values, far_mask, float(2**level_index)
        )
        numer = numer + jnp.repeat(numer_part[:, 0], 2**level_index, axis=1)
        denom = denom + jnp.repeat(denom_part[:, 0], 2**level_index, axis=1)
        far_saved.append((far_queries, far_keys, far_values, far_mask))
    attention = (
        (numer / denom[..., None]).astype(jnp.bfloat16).reshape(seq_count * row_count, features)
    )
    head_terms = jnp.dot(attention, w_out, preferred_element_type=jnp.float32)
    mixed = head_total(head_terms.reshape(seq_count, row_count, model_width)).astype(jnp.bfloat16)
    flat_grad = grad_y.reshape(seq_count * row_count, model_width)
    d_attention = jnp.einsum(
        "td,fd->tf", flat_grad, w_out, preferred_element_type=jnp.float32
    ).astype(jnp.bfloat16)
    norm_scale = 1.0 / math.sqrt(seq_count * row_count * seq_devices)
    wout_term = (
        jnp.einsum("td,tf->df", flat_grad, attention, preferred_element_type=jnp.float32)
        * norm_scale
    )
    attention_float = attention.astype(jnp.float32).reshape(seq_count, row_count, local_heads, HEAD)
    d_attention_float = d_attention.astype(jnp.float32).reshape(
        seq_count, row_count, local_heads, HEAD
    )
    inverse = 1.0 / denom
    pulled = d_attention_float * inverse[..., None]
    offset_sum = jnp.sum(d_attention_float * attention_float, axis=-1) * inverse
    near_dq, near_dk, near_dv = block_backward(
        near_queries,
        near_keys,
        near_values,
        near_mask,
        1.0,
        pulled.reshape(seq_count, 2, BLOCK, local_heads, HEAD),
        offset_sum.reshape(seq_count, 2, BLOCK, local_heads),
    )
    near_grad = joined(near_dk, near_dv)
    spread_grad = near_grad[:, 0] + near_grad[:, 1]
    from_next = send_back(spread_grad[:, :row_count], -1)
    from_prev = send_back(spread_grad[:, 2 * row_count :], 1)
    own_grad = spread_grad[:, row_count : 2 * row_count] + from_prev + from_next
    cotangents = [
        (
            near_dq.reshape(seq_count, row_count, local_heads, HEAD).astype(jnp.bfloat16),
            split_heads(own_grad, features, local_heads, 0).astype(jnp.bfloat16),
            split_heads(own_grad, features, local_heads, 1).astype(jnp.bfloat16),
        )
    ]
    for level_index in range(1, LEVELS):
        group_size = 2 ** (level_index - 1)
        factor = 2**level_index
        far_queries, far_keys, far_values, far_mask = far_saved[level_index - 1]
        own_count = far_queries.shape[2]
        level_pulled = pool_total(pulled, factor).reshape(
            seq_count, 1, own_count, local_heads, HEAD
        )
        level_offset = pool_total(offset_sum, factor).reshape(seq_count, 1, own_count, local_heads)
        far_dq, far_dk, far_dv = block_backward(
            far_queries, far_keys, far_values, far_mask, float(factor), level_pulled, level_offset
        )
        remote_grad = joined(far_dk[:, 0], far_dv[:, 0]).reshape(
            seq_count, len(FAR_OFFSETS), BLOCK, 2 * features
        )
        returned = jnp.zeros((seq_count, BLOCK, 2 * features), jnp.float32)
        for slot_index, offset in enumerate(FAR_OFFSETS):
            returned = returned + send_back(remote_grad[:, slot_index], offset * group_size)
        level_grad = split_sum(returned, group_size, 1, where_seq)
        cotangents.append(
            (
                far_dq[:, 0].astype(jnp.bfloat16),
                split_heads(level_grad, features, local_heads, 0).astype(jnp.bfloat16),
                split_heads(level_grad, features, local_heads, 1).astype(jnp.bfloat16),
            )
        )
    grads_pre = pull_back(tuple(cotangents))
    d_projected = (
        jnp.stack(grads_pre, axis=2)
        .astype(jnp.bfloat16)
        .reshape(seq_count * row_count, 3, features)
    )
    input_terms = jnp.einsum("tkc,kcd->td", d_projected, w_qkv, preferred_element_type=jnp.float32)
    grad_tokens = head_total(input_terms.reshape(seq_count, row_count, model_width)).astype(
        jnp.bfloat16
    )
    wqkv_term = (
        jnp.einsum("td,tkc->dkc", flat_tokens, d_projected, preferred_element_type=jnp.float32)
        * norm_scale
    )
    grad_wqkv, grad_wout = (
        lax.psum_scatter(wqkv_term, "seq", scatter_dimension=0, tiled=True),
        lax.psum_scatter(wout_term, "seq", scatter_dimension=0, tiled=True),
    )
    return (mixed, grad_tokens, grad_wqkv, grad_wout)


def solution(mesh):
    in_specs = (P(None, "seq", None), P(None, "mp", None), P("mp", None), P(None, "seq", None))
    out_specs = (P(None, "seq", "mp"), P(None, "seq", "mp"), P("seq", None, "mp"), P("seq", "mp"))
    return jax.shard_map(shards, mesh=mesh, in_specs=in_specs, out_specs=out_specs, check_vma=False)
```

profile of v0, /device:TPU:2, one launch (start us, length us, event | category | flops | bytes accessed | tf_op | source)
XLA Modules:
  0.0 445.1 jit_solution(3729128765489935206)
XLA Ops:
  9.2 1.4 convolution_bitcast_fusion.1
  14.4 2.9 collective-permute-start.2
  17.4 3.5 collective-permute-start.3
  20.8 1.3 collective-permute-start.4
  22.1 1.3 collective-permute-start.5
  39.9 3.0 collective-permute-start.12
  43.6 1.3 collective-permute-done.12
  44.9 1.3 collective-permute-start
  46.9 7.6 %collective-permute-start.7 = (bf16[1,128,384]{1,2,0:T(8,128)(2,1)}, bf16[1,128,384]{1,2,0:T(8,128)(2,1)}, u32[]{:S(2)}, u32[]{:S(2)}) collective-permute-start(bf16[1,128,384]{1,2,0:T(8,128)(2,1)} %maximum_select_fusion), channel_id=1, source_target_pairs={{0,24},{4,28},{8,32},{12,36},{16,40},{20,44},{24,48},{28,52},{32,5... | collective-permute-start | bytes 294920 | tf_op jit(solution)/shard_map/ppermute | solution.py:36
  54.5 5.9 %collective-permute-start.8 = (bf16[1,128,384]{1,2,0:T(8,128)(2,1)}, bf16[1,128,384]{1,2,0:T(8,128)(2,1)}, u32[]{:S(2)}, u32[]{:S(2)}) collective-permute-start(bf16[1,128,384]{1,2,0:T(8,128)(2,1)} %maximum_select_fusion), channel_id=1, source_target_pairs={{0,16},{4,20},{8,24},{12,28},{16,32},{20,36},{24,40},{28,44},{32,4... | collective-permute-start | bytes 294920 | tf_op jit(solution)/shard_map/ppermute | solution.py:36
  60.4 1.3 collective-permute-start.9
  61.7 1.5 collective-permute-start.10
  73.2 9.3 %collective-permute-start.13 = (bf16[1,128,384]{2,1,0:T(8,128)(2,1)}, bf16[1,128,384]{2,1,0:T(8,128)(2,1)S(1)}, u32[]{:S(2)}, u32[]{:S(2)}) collective-permute-start(bf16[1,128,384]{2,1,0:T(8,128)(2,1)} %maximum_select_fusion.1), channel_id=1, source_target_pairs={{0,48},{4,52},{8,56},{12,60},{16,64},{20,68},{24,72},{28,76},{32,8... | collective-permute-start | bytes 294920 | tf_op jit(solution)/shard_map/ppermute | solution.py:36
  82.5 3.2 collective-permute-start.14
  85.7 1.3 collective-permute-start.15
  87.0 1.3 collective-permute-start.16
  98.1 1.3 collective-permute-start.1
  115.2 1.3 multiply_reduce_fusion.6
  122.1 1.6 add_divide_fusion.1
  123.6 1.7 copy.540
  125.4 1.6 multiply_reduce_fusion.2
  132.2 1.2 fusion.24
  133.3 1.3 fusion.81
  134.7 1.4 fusion.37
  139.3 1.3 collective-permute-start.17
  140.6 1.3 collective-permute-start.18
  141.9 8.6 %collective-permute-start.19 = (bf16[1,128,384]{2,1,0:T(8,128)(2,1)}, bf16[1,128,384]{2,1,0:T(8,128)(2,1)}, u32[]{:S(2)}, u32[]{:S(2)}) collective-permute-start(bf16[1,128,384]{2,1,0:T(8,128)(2,1)} %get-tuple-element.59), channel_id=1, source_target_pairs={{0,32},{4,36},{8,40},{12,44},{16,48},{20,52},{24,56},{28,60},{32,6... | collective-permute-start | bytes 294920 | tf_op jit(solution)/shard_map/ppermute | solution.py:36
  150.5 7.8 %collective-permute-start.20 = (bf16[1,128,384]{2,1,0:T(8,128)(2,1)}, bf16[1,128,384]{2,1,0:T(8,128)(2,1)}, u32[]{:S(2)}, u32[]{:S(2)}) collective-permute-start(bf16[1,128,384]{2,1,0:T(8,128)(2,1)} %get-tuple-element.58), channel_id=1, source_target_pairs={{0,48},{4,52},{8,56},{12,60},{16,64},{20,68},{24,72},{28,76},{32,8... | collective-permute-start | bytes 294920 | tf_op jit(solution)/shard_map/ppermute | solution.py:36
  161.5 1.5 collective-permute-start.23
  169.2 1.4 multiply_reduce_fusion.11
  173.2 1.8 copy.582
  175.1 1.2 fusion.108
  181.0 1.3 collective-permute-start.24
  182.3 6.5 %collective-permute-start.25 = (bf16[1,128,384]{2,1,0:T(8,128)(2,1)S(1)}, bf16[1,128,384]{2,1,0:T(8,128)(2,1)S(1)}, u32[]{:S(2)}, u32[]{:S(2)}) collective-permute-start(bf16[1,128,384]{2,1,0:T(8,128)(2,1)S(1)} %copy-done.76), channel_id=1, source_target_pairs={{0,16},{4,20},{8,24},{12,28},{16,32},{20,36},{24,40},{28,44},{32,4... | collective-permute-start | bytes 294920 | tf_op jit(solution)/shard_map/ppermute | solution.py:36
  188.8 6.7 %collective-permute-start.26 = (bf16[1,128,384]{2,1,0:T(8,128)(2,1)S(1)}, bf16[1,128,384]{2,1,0:T(8,128)(2,1)S(1)}, u32[]{:S(2)}, u32[]{:S(2)}) collective-permute-start(bf16[1,128,384]{2,1,0:T(8,128)(2,1)S(1)} %copy-done.74), channel_id=1, source_target_pairs={{0,24},{4,28},{8,32},{12,36},{16,40},{20,44},{24,48},{28,52},{32,5... | collective-permute-start | bytes 294920 | tf_op jit(solution)/shard_map/ppermute | solution.py:36
  195.5 1.3 collective-permute-start.28
  198.0 1.3 collective-permute-start.29
  199.3 4.6 %collective-permute-start.30 = (bf16[1,128,384]{1,2,0:T(8,128)(2,1)S(1)}, bf16[1,128,384]{1,2,0:T(8,128)(2,1)S(1)}, u32[]{:S(2)}, u32[]{:S(2)}) collective-permute-start(bf16[1,128,384]{1,2,0:T(8,128)(2,1)S(1)} %copy-done.77), channel_id=1, source_target_pairs={{0,8},{4,12},{8,16},{12,20},{16,24},{20,28},{24,32},{28,36},{32,40... | collective-permute-start | bytes 294920 | tf_op jit(solution)/shard_map/ppermute | solution.py:36
  203.9 3.7 collective-permute-start.31
  207.6 3.9 collective-permute-start.32
  212.5 1.3 collective-permute-start.33
  213.8 3.6 collective-permute-start.21
  217.8 4.1 collective-permute-done.21
  226.6 1.2 fusion.40
  233.8 2.8 copy.608
  240.2 16.7 %reduce-scatter.10.cloned.1.call-done = bf16[192,256]{1,0:T(8,128)(2,1)} async-done(((bf16[768,256]{1,0:T(8,128)(2,1)}), bf16[192,256]{1,0:T(8,128)(2,1)}) %reduce-scatter.10.cloned.1.call-update) | async-done | bytes 98320
  258.6 176.0 %all-reduce.5.cloned.1.call-done = (f32[768,3,192]{2,1,0:T(4,128)}, f32[768,192]{0,1:T(8,128)}) async-done(((f32[768,3,192]{2,1,0:T(4,128)}, f32[768,192]{0,1:T(8,128)}), (f32[768,3,192]{2,1,0:T(4,128)}, f32[768,192]{0,1:T(8,128)})) %all-reduce.5.cloned.1.call-update) | async-done | bytes 2359312
  436.3 1.4 constant_dynamic-slice_fusion.1
  (609 shorter events, 106.0 us)
Async XLA Ops:
  8.0 230.5 %reduce-scatter.8.cloned.1.call-start = ((), (), s32[]{:S(2)}) async-start(), calls=%async_computation.2 | async-start | bytes 491520
  14.4 32.5 %collective-permute-start.2 = (bf16[1,128,384]{1,2,0:T(8,128)(2,1)}, bf16[1,128,384]{1,2,0:T(8,128)(2,1)S(1)}, u32[]{:S(2)}, u32[]{:S(2)}) collective-permute-start(bf16[1,128,384]{1,2,0:T(8,128)(2,1)} %pad_maximum_fusion.9), channel_id=1, source_target_pairs={{0,12},{4,16},{8,20},{12,24},{16,28},{20,32},{24,36},{28,40},{32,4... | collective-permute-start | bytes 294920 | tf_op jit(solution)/shard_map/ppermute | solution.py:36
  17.4 37.1 %collective-permute-start.3 = (bf16[1,128,384]{1,2,0:T(8,128)(2,1)}, bf16[1,128,384]{1,2,0:T(8,128)(2,1)S(1)}, u32[]{:S(2)}, u32[]{:S(2)}) collective-permute-start(bf16[1,128,384]{1,2,0:T(8,128)(2,1)} %pad_maximum_fusion.9), channel_id=1, source_target_pairs={{0,8},{4,12},{8,16},{12,20},{16,24},{20,28},{24,32},{28,36},{32,40... | collective-permute-start | bytes 294920 | tf_op jit(solution)/shard_map/ppermute | solution.py:36
  20.8 39.5 %collective-permute-start.4 = (bf16[1,128,384]{1,2,0:T(8,128)(2,1)}, bf16[1,128,384]{1,2,0:T(8,128)(2,1)S(1)}, u32[]{:S(2)}, u32[]{:S(2)}) collective-permute-start(bf16[1,128,384]{1,2,0:T(8,128)(2,1)} %pad_maximum_fusion.9), channel_id=1, source_target_pairs={{8,0},{12,4},{16,8},{20,12},{24,16},{28,20},{32,24},{36,28},{40,32... | collective-permute-start | bytes 294920 | tf_op jit(solution)/shard_map/ppermute | solution.py:36
  22.1 39.5 %collective-permute-start.5 = (bf16[1,128,384]{1,2,0:T(8,128)(2,1)}, bf16[1,128,384]{1,2,0:T(8,128)(2,1)S(1)}, u32[]{:S(2)}, u32[]{:S(2)}) collective-permute-start(bf16[1,128,384]{1,2,0:T(8,128)(2,1)} %pad_maximum_fusion.9), channel_id=1, source_target_pairs={{12,0},{16,4},{20,8},{24,12},{28,16},{32,20},{36,24},{40,28},{44,3... | collective-permute-start | bytes 294920 | tf_op jit(solution)/shard_map/ppermute | solution.py:36
  26.6 12.0 %collective-permute-start.11 = (bf16[1,32,384]{2,1,0:T(8,128)(2,1)S(1)}, bf16[1,32,384]{2,1,0:T(8,128)(2,1)S(1)}, u32[]{:S(2)}, u32[]{:S(2)}) collective-permute-start(bf16[1,32,384]{2,1,0:T(8,128)(2,1)S(1)} %pad_maximum_fusion.11), channel_id=1, source_target_pairs={{0,4},{4,0},{8,12},{12,8},{16,20},{20,16},{24,28},{28,24},{32,36},... | collective-permute-start | bytes 73736 | tf_op jit(solution)/shard_map/ppermute | solution.py:30
  28.0 80.7 %copy-start.89 = (f32[2,128,3]{1,2,0:T(4,128)}, f32[2,128,3]{1,2,0:T(4,128)S(1)}, u32[]{:S(2)}) copy-start(f32[2,128,3]{1,2,0:T(4,128)S(1)} %get-tuple-element.77) | copy-start | bytes 9220
  30.0 33.9 %copy-start.97 = (f32[128,3]{0,1:T(4,128)}, f32[128,3]{0,1:T(4,128)S(1)}, u32[]{:S(2)}) copy-start(f32[128,3]{0,1:T(4,128)S(1)} %get-tuple-element.80) | copy-start | bytes 4612
  30.8 59.3 %copy-start.21 = (f32[64,3,64]{2,0,1:T(8,128)}, f32[64,3,64]{2,0,1:T(8,128)S(1)}, u32[]{:S(2)}) copy-start(f32[64,3,64]{2,0,1:T(8,128)S(1)} %multiply_reduce_fusion.7) | copy-start | bytes 147460
  31.6 58.5 %copy-start.99 = (f32[64,3]{0,1:T(4,128)}, f32[64,3]{0,1:T(4,128)S(1)}, u32[]{:S(2)}) copy-start(f32[64,3]{0,1:T(4,128)S(1)} %get-tuple-element.82) | copy-start | bytes 2308
  31.9 69.4 %copy-start.37 = (f32[32,3,64]{2,0,1:T(8,128)}, f32[32,3,64]{2,0,1:T(8,128)S(1)}, u32[]{:S(2)}) copy-start(f32[32,3,64]{2,0,1:T(8,128)S(1)} %multiply_reduce_fusion.14) | copy-start | bytes 73732
  32.7 68.7 %copy-start.103 = (f32[32,3]{0,1:T(4,128)}, f32[32,3]{0,1:T(4,128)S(1)}, u32[]{:S(2)}) copy-start(f32[32,3]{0,1:T(4,128)S(1)} %get-tuple-element.84) | copy-start | bytes 1156
  38.6 1.3 collective-permute-start.6
  39.9 5.1 %collective-permute-start.12 = (bf16[1,64,384]{2,1,0:T(8,128)(2,1)S(1)}, bf16[1,64,384]{2,1,0:T(8,128)(2,1)S(1)}, u32[]{:S(2)}, u32[]{:S(2)}) collective-permute-start(bf16[1,64,384]{2,1,0:T(8,128)(2,1)S(1)} %maximum_select_fusion.3), channel_id=1, source_target_pairs={{0,8},{4,12},{8,0},{12,4},{16,24},{20,28},{24,16},{28,20},{32,40},... | collective-permute-start | bytes 147464 | tf_op jit(solution)/shard_map/ppermute | solution.py:30
  44.9 63.7 %collective-permute-start = (bf16[1,256,384]{1,2,0:T(8,128)(2,1)S(1)}, bf16[1,256,384]{1,2,0:T(8,128)(2,1)S(1)}, u32[]{:S(2)}, u32[]{:S(2)}) collective-permute-start(bf16[1,256,384]{1,2,0:T(8,128)(2,1)S(1)} %pad_maximum_fusion.6), channel_id=1, source_target_pairs={{0,4},{4,8},{8,12},{12,16},{16,20},{20,24},{24,28},{28,32},{32,36}... | collective-permute-start | bytes 589832 | tf_op jit(solution)/shard_map/ppermute | solution.py:44
  46.9 26.3 %collective-permute-start.7 = (bf16[1,128,384]{1,2,0:T(8,128)(2,1)}, bf16[1,128,384]{1,2,0:T(8,128)(2,1)}, u32[]{:S(2)}, u32[]{:S(2)}) collective-permute-start(bf16[1,128,384]{1,2,0:T(8,128)(2,1)} %maximum_select_fusion), channel_id=1, source_target_pairs={{0,24},{4,28},{8,32},{12,36},{16,40},{20,44},{24,48},{28,52},{32,5... | collective-permute-start | bytes 294920 | tf_op jit(solution)/shard_map/ppermute | solution.py:36
  54.5 28.0 %collective-permute-start.8 = (bf16[1,128,384]{1,2,0:T(8,128)(2,1)}, bf16[1,128,384]{1,2,0:T(8,128)(2,1)}, u32[]{:S(2)}, u32[]{:S(2)}) collective-permute-start(bf16[1,128,384]{1,2,0:T(8,128)(2,1)} %maximum_select_fusion), channel_id=1, source_target_pairs={{0,16},{4,20},{8,24},{12,28},{16,32},{20,36},{24,40},{28,44},{32,4... | collective-permute-start | bytes 294920 | tf_op jit(solution)/shard_map/ppermute | solution.py:36
  60.4 25.3 %collective-permute-start.9 = (bf16[1,128,384]{1,2,0:T(8,128)(2,1)}, bf16[1,128,384]{1,2,0:T(8,128)(2,1)}, u32[]{:S(2)}, u32[]{:S(2)}) collective-permute-start(bf16[1,128,384]{1,2,0:T(8,128)(2,1)} %maximum_select_fusion), channel_id=1, source_target_pairs={{16,0},{20,4},{24,8},{28,12},{32,16},{36,20},{40,24},{44,28},{48,3... | collective-permute-start | bytes 294920 | tf_op jit(solution)/shard_map/ppermute | solution.py:36
  61.7 25.3 %collective-permute-start.10 = (bf16[1,128,384]{1,2,0:T(8,128)(2,1)}, bf16[1,128,384]{1,2,0:T(8,128)(2,1)}, u32[]{:S(2)}, u32[]{:S(2)}) collective-permute-start(bf16[1,128,384]{1,2,0:T(8,128)(2,1)} %maximum_select_fusion), channel_id=1, source_target_pairs={{24,0},{28,4},{32,8},{36,12},{40,16},{44,20},{48,24},{52,28},{56,3... | collective-permute-start | bytes 294920 | tf_op jit(solution)/shard_map/ppermute | solution.py:36
  73.2 24.9 %collective-permute-start.13 = (bf16[1,128,384]{2,1,0:T(8,128)(2,1)}, bf16[1,128,384]{2,1,0:T(8,128)(2,1)S(1)}, u32[]{:S(2)}, u32[]{:S(2)}) collective-permute-start(bf16[1,128,384]{2,1,0:T(8,128)(2,1)} %maximum_select_fusion.1), channel_id=1, source_target_pairs={{0,48},{4,52},{8,56},{12,60},{16,64},{20,68},{24,72},{28,76},{32,8... | collective-permute-start | bytes 294920 | tf_op jit(solution)/shard_map/ppermute | solution.py:36
  82.5 16.9 %collective-permute-start.14 = (bf16[1,128,384]{2,1,0:T(8,128)(2,1)}, bf16[1,128,384]{2,1,0:T(8,128)(2,1)S(1)}, u32[]{:S(2)}, u32[]{:S(2)}) collective-permute-start(bf16[1,128,384]{2,1,0:T(8,128)(2,1)} %maximum_select_fusion.1), channel_id=1, source_target_pairs={{0,32},{4,36},{8,40},{12,44},{16,48},{20,52},{24,56},{28,60},{32,6... | collective-permute-start | bytes 294920 | tf_op jit(solution)/shard_map/ppermute | solution.py:36
  85.7 13.7 %collective-permute-start.15 = (bf16[1,128,384]{2,1,0:T(8,128)(2,1)}, bf16[1,128,384]{2,1,0:T(8,128)(2,1)}, u32[]{:S(2)}, u32[]{:S(2)}) collective-permute-start(bf16[1,128,384]{2,1,0:T(8,128)(2,1)} %maximum_select_fusion.1), channel_id=1, source_target_pairs={{32,0},{36,4},{40,8},{44,12},{48,16},{52,20},{56,24},{60,28},{64,3... | collective-permute-start | bytes 294920 | tf_op jit(solution)/shard_map/ppermute | solution.py:36
  87.0 13.1 %collective-permute-start.16 = (bf16[1,128,384]{2,1,0:T(8,128)(2,1)}, bf16[1,128,384]{2,1,0:T(8,128)(2,1)}, u32[]{:S(2)}, u32[]{:S(2)}) collective-permute-start(bf16[1,128,384]{2,1,0:T(8,128)(2,1)} %maximum_select_fusion.1), channel_id=1, source_target_pairs={{48,0},{52,4},{56,8},{60,12},{64,16},{68,20},{72,24},{76,28},{80,3... | collective-permute-start | bytes 294920 | tf_op jit(solution)/shard_map/ppermute | solution.py:36
  98.1 10.5 %collective-permute-start.1 = (bf16[1,256,384]{1,2,0:T(8,128)(2,1)S(1)}, bf16[1,256,384]{1,2,0:T(8,128)(2,1)S(1)}, u32[]{:S(2)}, u32[]{:S(2)}) collective-permute-start(bf16[1,256,384]{1,2,0:T(8,128)(2,1)S(1)} %pad_maximum_fusion.6), channel_id=1, source_target_pairs={{4,0},{8,4},{12,8},{16,12},{20,16},{24,20},{28,24},{32,28},{36,32}... | collective-permute-start | bytes 589832 | tf_op jit(solution)/shard_map/ppermute | solution.py:47
  138.6 20.7 %copy-start.69 = (f32[1,64,4,3]{2,1,3,0:T(8,128)S(1)}, f32[1,64,4,3]{2,1,3,0:T(8,128)}, u32[]{:S(2)}) copy-start(f32[1,64,4,3]{2,1,3,0:T(8,128)} %copy.558) | copy-start | bytes 9220
  138.6 20.7 %copy-start.71 = (f32[1,64,4,3]{2,1,3,0:T(8,128)S(1)}, f32[1,64,4,3]{2,1,3,0:T(8,128)}, u32[]{:S(2)}) copy-start(f32[1,64,4,3]{2,1,3,0:T(8,128)} %reduce_sum.415) | copy-start | bytes 9220
  138.6 20.7 %copy-start.72 = (f32[1,64,4,3]{2,1,3,0:T(8,128)S(1)}, f32[1,64,4,3]{2,1,3,0:T(8,128)}, u32[]{:S(2)}) copy-start(f32[1,64,4,3]{2,1,3,0:T(8,128)} %reshape.2451) | copy-start | bytes 9220
  138.6 20.9 %copy-start.36 = (bf16[1,1,512,192]{2,3,1,0:T(8,128)(2,1)S(1)}, bf16[1,1,512,192]{2,3,1,0:T(8,128)(2,1)}, u32[]{:S(2)}) copy-start(bf16[1,1,512,192]{2,3,1,0:T(8,128)(2,1)} %copy-done.35) | copy-start | bytes 589828
  139.3 41.6 %collective-permute-start.17 = (bf16[1,128,384]{2,1,0:T(8,128)(2,1)}, bf16[1,128,384]{2,1,0:T(8,128)(2,1)}, u32[]{:S(2)}, u32[]{:S(2)}) collective-permute-start(bf16[1,128,384]{2,1,0:T(8,128)(2,1)} %get-tuple-element.57), channel_id=1, source_target_pairs={{48,0},{52,4},{56,8},{60,12},{64,16},{68,20},{72,24},{76,28},{80,3... | collective-permute-start | bytes 294920 | tf_op jit(solution)/shard_map/ppermute | solution.py:36
  140.6 41.7 %collective-permute-start.18 = (bf16[1,128,384]{2,1,0:T(8,128)(2,1)}, bf16[1,128,384]{2,1,0:T(8,128)(2,1)}, u32[]{:S(2)}, u32[]{:S(2)}) collective-permute-start(bf16[1,128,384]{2,1,0:T(8,128)(2,1)} %get-tuple-element.60), channel_id=1, source_target_pairs={{32,0},{36,4},{40,8},{44,12},{48,16},{52,20},{56,24},{60,28},{64,3... | collective-permute-start | bytes 294920 | tf_op jit(solution)/shard_map/ppermute | solution.py:36
  141.9 46.9 %collective-permute-start.19 = (bf16[1,128,384]{2,1,0:T(8,128)(2,1)}, bf16[1,128,384]{2,1,0:T(8,128)(2,1)}, u32[]{:S(2)}, u32[]{:S(2)}) collective-permute-start(bf16[1,128,384]{2,1,0:T(8,128)(2,1)} %get-tuple-element.59), channel_id=1, source_target_pairs={{0,32},{4,36},{8,40},{12,44},{16,48},{20,52},{24,56},{28,60},{32,6... | collective-permute-start | bytes 294920 | tf_op jit(solution)/shard_map/ppermute | solution.py:36
  150.5 45.0 %collective-permute-start.20 = (bf16[1,128,384]{2,1,0:T(8,128)(2,1)}, bf16[1,128,384]{2,1,0:T(8,128)(2,1)}, u32[]{:S(2)}, u32[]{:S(2)}) collective-permute-start(bf16[1,128,384]{2,1,0:T(8,128)(2,1)} %get-tuple-element.58), channel_id=1, source_target_pairs={{0,48},{4,52},{8,56},{12,60},{16,64},{20,68},{24,72},{28,76},{32,8... | collective-permute-start | bytes 294920 | tf_op jit(solution)/shard_map/ppermute | solution.py:36
  161.5 36.4 %collective-permute-start.23 = (bf16[1,128,384]{2,1,0:T(8,128)(2,1)}, bf16[1,128,384]{2,1,0:T(8,128)(2,1)}, u32[]{:S(2)}, u32[]{:S(2)}) collective-permute-start(bf16[1,128,384]{2,1,0:T(8,128)(2,1)} %get-tuple-element.53), channel_id=1, source_target_pairs={{24,0},{28,4},{32,8},{36,12},{40,16},{44,20},{48,24},{52,28},{56,3... | collective-permute-start | bytes 294920 | tf_op jit(solution)/shard_map/ppermute | solution.py:36
  180.0 23.8 %copy-start.75 = (bf16[1,128,384]{1,2,0:T(8,128)(2,1)S(1)}, bf16[1,128,384]{1,2,0:T(8,128)(2,1)}, u32[]{:S(2)}) copy-start(bf16[1,128,384]{1,2,0:T(8,128)(2,1)} %get-tuple-element.50) | copy-start | bytes 294916
  180.9 76.0 %reduce-scatter.10.cloned.1.call-start = ((), (), s32[]{:S(2)}) async-start(), calls=%async_computation.3 | async-start | bytes 491520
  181.0 18.3 %collective-permute-start.24 = (bf16[1,128,384]{2,1,0:T(8,128)(2,1)S(1)}, bf16[1,128,384]{2,1,0:T(8,128)(2,1)S(1)}, u32[]{:S(2)}, u32[]{:S(2)}) collective-permute-start(bf16[1,128,384]{2,1,0:T(8,128)(2,1)S(1)} %copy-done.78), channel_id=1, source_target_pairs={{16,0},{20,4},{24,8},{28,12},{32,16},{36,20},{40,24},{44,28},{48,3... | collective-permute-start | bytes 294920 | tf_op jit(solution)/shard_map/ppermute | solution.py:36
  182.3 21.5 %collective-permute-start.25 = (bf16[1,128,384]{2,1,0:T(8,128)(2,1)S(1)}, bf16[1,128,384]{2,1,0:T(8,128)(2,1)S(1)}, u32[]{:S(2)}, u32[]{:S(2)}) collective-permute-start(bf16[1,128,384]{2,1,0:T(8,128)(2,1)S(1)} %copy-done.76), channel_id=1, source_target_pairs={{0,16},{4,20},{8,24},{12,28},{16,32},{20,36},{24,40},{28,44},{32,4... | collective-permute-start | bytes 294920 | tf_op jit(solution)/shard_map/ppermute | solution.py:36
  188.8 18.8 %collective-permute-start.26 = (bf16[1,128,384]{2,1,0:T(8,128)(2,1)S(1)}, bf16[1,128,384]{2,1,0:T(8,128)(2,1)S(1)}, u32[]{:S(2)}, u32[]{:S(2)}) collective-permute-start(bf16[1,128,384]{2,1,0:T(8,128)(2,1)S(1)} %copy-done.74), channel_id=1, source_target_pairs={{0,24},{4,28},{8,32},{12,36},{16,40},{20,44},{24,48},{28,52},{32,5... | collective-permute-start | bytes 294920 | tf_op jit(solution)/shard_map/ppermute | solution.py:36
  195.5 16.9 %collective-permute-start.28 = (bf16[1,128,384]{1,2,0:T(8,128)(2,1)S(1)}, bf16[1,128,384]{1,2,0:T(8,128)(2,1)S(1)}, u32[]{:S(2)}, u32[]{:S(2)}) collective-permute-start(bf16[1,128,384]{1,2,0:T(8,128)(2,1)S(1)} %copy-done.80), channel_id=1, source_target_pairs={{12,0},{16,4},{20,8},{24,12},{28,16},{32,20},{36,24},{40,28},{44,3... | collective-permute-start | bytes 294920 | tf_op jit(solution)/shard_map/ppermute | solution.py:36
  198.0 15.8 %collective-permute-start.29 = (bf16[1,128,384]{1,2,0:T(8,128)(2,1)S(1)}, bf16[1,128,384]{1,2,0:T(8,128)(2,1)S(1)}, u32[]{:S(2)}, u32[]{:S(2)}) collective-permute-start(bf16[1,128,384]{1,2,0:T(8,128)(2,1)S(1)} %copy-done.79), channel_id=1, source_target_pairs={{8,0},{12,4},{16,8},{20,12},{24,16},{28,20},{32,24},{36,28},{40,32... | collective-permute-start | bytes 294920 | tf_op jit(solution)/shard_map/ppermute | solution.py:36
  199.3 18.1 %collective-permute-start.30 = (bf16[1,128,384]{1,2,0:T(8,128)(2,1)S(1)}, bf16[1,128,384]{1,2,0:T(8,128)(2,1)S(1)}, u32[]{:S(2)}, u32[]{:S(2)}) collective-permute-start(bf16[1,128,384]{1,2,0:T(8,128)(2,1)S(1)} %copy-done.77), channel_id=1, source_target_pairs={{0,8},{4,12},{8,16},{12,20},{16,24},{20,28},{24,32},{28,36},{32,40... | collective-permute-start | bytes 294920 | tf_op jit(solution)/shard_map/ppermute | solution.py:36
  203.9 13.7 %collective-permute-start.31 = (bf16[1,128,384]{1,2,0:T(8,128)(2,1)S(1)}, bf16[1,128,384]{1,2,0:T(8,128)(2,1)S(1)}, u32[]{:S(2)}, u32[]{:S(2)}) collective-permute-start(bf16[1,128,384]{1,2,0:T(8,128)(2,1)S(1)} %copy-done.75), channel_id=1, source_target_pairs={{0,12},{4,16},{8,20},{12,24},{16,28},{20,32},{24,36},{28,40},{32,4... | collective-permute-start | bytes 294920 | tf_op jit(solution)/shard_map/ppermute | solution.py:36
  207.6 18.9 %collective-permute-start.32 = (bf16[1,256,384]{1,2,0:T(8,128)(2,1)}, bf16[1,256,384]{1,2,0:T(8,128)(2,1)}, u32[]{:S(2)}, u32[]{:S(2)}) collective-permute-start(bf16[1,256,384]{1,2,0:T(8,128)(2,1)} %get-tuple-element.42), channel_id=1, source_target_pairs={{0,4},{4,8},{8,12},{12,16},{16,20},{20,24},{24,28},{28,32},{32,36}... | collective-permute-start | bytes 589832 | tf_op jit(solution)/shard_map/ppermute | solution.py:36
  212.5 14.1 %collective-permute-start.33 = (bf16[1,256,384]{1,2,0:T(8,128)(2,1)}, bf16[1,256,384]{1,2,0:T(8,128)(2,1)}, u32[]{:S(2)}, u32[]{:S(2)}) collective-permute-start(bf16[1,256,384]{1,2,0:T(8,128)(2,1)} %get-tuple-element.43), channel_id=1, source_target_pairs={{4,0},{8,4},{12,8},{16,12},{20,16},{24,20},{28,24},{32,28},{36,32}... | collective-permute-start | bytes 589832 | tf_op jit(solution)/shard_map/ppermute | solution.py:36
  213.8 8.1 %collective-permute-start.21 = (bf16[1,64,384]{2,1,0:T(8,128)(2,1)S(1)}, bf16[1,64,384]{2,1,0:T(8,128)(2,1)S(1)}, u32[]{:S(2)}, u32[]{:S(2)}) collective-permute-start(bf16[1,64,384]{2,1,0:T(8,128)(2,1)S(1)} %select_convert_fusion.1), channel_id=1, source_target_pairs={{0,8},{4,12},{8,0},{12,4},{16,24},{20,28},{24,16},{28,20},{32,40},... | collective-permute-start | bytes 147464 | tf_op jit(solution)/shard_map/ppermute | solution.py:30
  217.3 4.7 %collective-permute-start.27 = (bf16[1,64,384]{2,1,0:T(8,128)(2,1)S(1)}, bf16[1,64,384]{2,1,0:T(8,128)(2,1)S(1)}, u32[]{:S(2)}, u32[]{:S(2)}) collective-permute-start(bf16[1,64,384]{2,1,0:T(8,128)(2,1)S(1)} %select_convert_fusion), channel_id=1, source_target_pairs={{0,4},{4,0},{8,12},{12,8},{16,20},{20,16},{24,28},{28,24},{32,36},... | collective-permute-start | bytes 147464 | tf_op jit(solution)/shard_map/ppermute | solution.py:30
  221.9 1.3 collective-permute-start.22
  231.1 203.5 %all-reduce.5.cloned.1.call-start = ((), (), s32[]{:S(2)}) async-start(), calls=%async_computation.4 | async-start | bytes 7471104
  (125 other events, 532.6 us)
Sparse Core Ops, SparseCore 0:
  181.0 27.9 reduce-scatter.7
  231.2 25.6 reduce-scatter.9
Sparse Core Ops, SparseCore 1:
  236.7 197.8 all-reduce.4
where the time goes:
time: 447 us; the launch traced here: 445 us
  waiting for transfers between devices  201 us (45%)
  starting transfers between devices  102 us (23%)
  local copies, waits for them, and re-layouts  79.2 us (18%)
  other arithmetic  26.5 us (6%)
  between operations  19.3 us (4%)
  matrix products  17.3 us (4%)
    unnamed x6, waiting for transfers between devices  193 us
    ppermute x26, starting transfers between devices, shifted(): lax.ppermute(value, axis, [(source, source + steps) for source in range(l...  91.3 us
    unnamed x292, local copies, waits for them, and re-layouts  19.6 us
    broadcast_in_dim x25, local copies, waits for them, and re-layouts, shards(): denom = denom + jnp.repeat(denom_part[:, 0], 2 ** level_index, axis=1)  13.1 us
  transfers between devices with their start and end apart: 37, of which 7 were waited for; matrix products, arithmetic and copies ran while one was open for 18% of the time, Pallas kernels for 0%

commit v1 on v0

v1 whole, which is shorter than its diff:
```python
import jax
import jax.numpy as jnp
from jax import lax
from jax.experimental import pallas as pl
from jax.experimental.pallas import tpu as pltpu
from jax.sharding import PartitionSpec as P

F32 = jnp.float32
BF16 = jnp.bfloat16
MESH = pl.DeviceIdType.MESH
EPS = 1e-06
ROOT_HALF = 0.7071067811865476
NORM = 1.0 / 128.0
WINDOWS = (0, 128, 384, 512)


def nn(a, b):
    return jnp.dot(a, b, preferred_element_type=F32)


def nt(a, b):
    return lax.dot_general(a, b, (((1,), (1,)), ((), ())), preferred_element_type=F32)


def unit_parts(x):
    heads = x.reshape(x.shape[0] // 64, 64, x.shape[1])
    scale = lax.rsqrt(jnp.mean(heads * heads, axis=1, keepdims=True) + EPS)
    return heads * scale, scale


def unit(x):
    return unit_parts(x)[0].reshape(x.shape)


def unit_back(x, grad):
    y, scale = unit_parts(x)
    dy = grad.reshape(y.shape)
    return (scale * (dy - y * jnp.mean(y * dy, axis=1, keepdims=True))).reshape(x.shape)


def round_low(x):
    return x.astype(BF16).astype(F32)


def iota(shape, dim):
    return lax.broadcasted_iota(jnp.int32, shape, dim)


def one_hot(cond):
    return jnp.where(cond, 1.0, 0.0).astype(BF16)


def natural_token(row):
    high = row >> 5
    return (row & 31) * 8 + (((high & 1) << 2) | (high & 2) | ((high >> 2) & 1))


def kernel(
    tok_ref, wqkv_ref, wout_ref, gy_ref,
    mixed_ref, gt_ref, oa_ref, ob_ref,
    permt, u0, uc, kv0, kvc, ownc, kvt0, kvtc, w0, wc, qm0, qmc, gm0, gmc, c0, cc,
    num0, numc, den0, denc, dot_s, att_s, dq0, dqc, down, dsend0, dsendc, ret0, retc,
    tg, ptg, ra, pra, dkvt, pdkvt, mixs, mixr, gtacc, gts, gtr,
    gf, gs, yr, zs, zr,
    fs_sem, fr_sem, bs_sem, br_sem, cs_sem, cr_sem, ms_sem, mr_sem, ys_sem, yr_sem, zs_sem, zr_sem,
):
    s = lax.axis_index("seq")
    m = lax.axis_index("mp")
    core = lax.rem(s, 2)
    y = lax.rem(s // 2, 4)
    z = s // 8
    position = (s, s // 2, s // 4)
    extent = (64, 32, 16)
    skip = [3 - 6 * lax.rem(position[lv], 2) for lv in range(3)]

    def offset(lv, j):
        return (-2, 2, skip[lv])[j]

    def target(lv, j, part):
        block = lax.rem(position[lv] + offset(lv, j) + extent[lv], extent[lv])
        return block * (1 << lv) + part

    def back_slot(j):
        return (1, 0, 2)[j]

    prev_dev = lax.rem(s + 63, 64)
    next_dev = lax.rem(s + 1, 64)
    peer = s + 1 - 2 * core

    def y_dev(k):
        return z * 8 + lax.rem(y + k, 4) * 2 + core

    def z_dev(k):
        return lax.rem(z + k, 8) * 8 + y * 2 + core

    def mp_dev(k):
        return lax.rem(m + k, 4)

    barrier = pltpu.get_barrier_semaphore()
    partners = [{"seq": prev_dev}, {"seq": next_dev}]
    for lv in range(3):
        for j in range(3):
            for part in range(1 << lv):
                partners.append({"seq": target(lv, j, part)})
    partners += [{"seq": y_dev(k)} for k in range(1, 4)]
    partners += [{"seq": z_dev(k)} for k in range(1, 8)]
    partners += [{"mp": mp_dev(k)} for k in range(1, 4)]
    partners += [{"seq": peer}]
    for partner in partners:
        pl.semaphore_signal(barrier, inc=1, device_id=partner, device_id_type=MESH)

    def remote(src, dst, send, recv, where):
        return pltpu.make_async_remote_copy(
            src_ref=src, dst_ref=dst, send_sem=send, recv_sem=recv,
            device_id=where, device_id_type=MESH,
        )

    row = iota((256, 256), 0)
    col = iota((256, 256), 1)
    perm = one_hot(natural_token(row) == col)
    permt[...] = one_hot(natural_token(col) == row)
    tok_p = nn(perm, tok_ref[...]).astype(BF16)
    u0[...] = nt(wqkv_ref[...], tok_p)

    def store_q(dst, q_rows, n):
        dst[...] = jnp.zeros(dst.shape, BF16)
        half = (q_rows * 0.5).astype(BF16)
        for h in range(3):
            dst[64 * h : 64 * h + 64, h * n : h * n + n] = half[64 * h : 64 * h + 64]

    qk = unit(u0[0:384, :])
    v = u0[384:576, :]
    store_q(qm0, qk[0:192], 256)
    kv0[1] = jnp.concatenate([qk[192:384], v], axis=0).T.astype(BF16)
    for lv in range(3):
        if lv == 0:
            mean = (qk[:, 0:128] + qk[:, 128:256]) * 0.5
            v = (v[:, 0:128] + v[:, 128:256]) * ROOT_HALF
        else:
            mean = (qk + pltpu.roll(qk, 128 >> lv, 1)) * 0.5
            v = (v + pltpu.roll(v, 128 >> lv, 1)) * ROOT_HALF
        uc[lv] = mean
        qk = unit(mean)
        store_q(qmc.at[lv], qk[0:192], 128)
        ownc[lv] = jnp.concatenate([qk[192:384], v], axis=0).T.astype(BF16)

    pl.semaphore_wait(barrier, len(partners))

    for lv in range(3):
        rows = 128 >> lv
        mine = lax.rem(s, 1 << lv) * rows
        for j in range(3):
            i = 3 * lv + back_slot(j)
            for part in range(1 << lv):
                remote(
                    ownc.at[lv, pl.ds(0, rows)],
                    kvc.at[i, pl.ds(mine, rows)],
                    fs_sem.at[i], fr_sem.at[i], {"seq": target(lv, j, part)},
                ).start()
    remote(kv0.at[1], kv0.at[0], fs_sem.at[9], fr_sem.at[9], {"seq": next_dev}).start()
    remote(kv0.at[1], kv0.at[2], fs_sem.at[10], fr_sem.at[10], {"seq": prev_dev}).start()

    num0[...] = jnp.zeros(num0.shape, F32)
    numc[...] = jnp.zeros(numc.shape, F32)
    den0[...] = jnp.zeros(den0.shape, F32)
    denc[...] = jnp.zeros(denc.shape, F32)
    dq0[...] = jnp.zeros(dq0.shape, F32)
    dqc[...] = jnp.zeros(dqc.shape, F32)
    ra[...] = jnp.zeros(ra.shape, BF16)
    pra[0:192, 256:512] = jnp.zeros((192, 256), BF16)
    pra[192:384, 0:256] = jnp.zeros((192, 256), BF16)

    def forward(keys, keyst, qm, w_ref, num, den, factor, n):
        block = keys[...]
        count = block.shape[0]
        keyst[...] = block.astype(F32).T.astype(BF16)
        for h in range(3):
            lanes = slice(h * n, h * n + n)
            w = jnp.exp(nn(block[:, 0:256], qm[:, lanes])) * factor
            den[:, lanes] += jnp.sum(w.reshape(count // 8, 8, n), axis=0)
            wb = w.astype(BF16)
            w_ref[:, lanes] = wb
            num[64 * h : 64 * h + 64, :] += nn(keyst[192 + 64 * h : 256 + 64 * h, :], wb)

    def keep0(j):
        if j == 1:
            return jnp.float32(1.0)
        inside = s > 0 if j == 0 else s < 63
        return jnp.where(inside, jnp.float32(1.0), jnp.float32(0.0))

    forward(kv0.at[1], kvt0.at[1], qm0, w0.at[1], num0, den0, keep0(1), 256)

    gy_p = nn(perm, gy_ref[...]).astype(BF16)
    dot_s[...] = nt(wout_ref[...], gy_p).astype(BF16)
    for half in range(2):
        index = iota((384, 768), 0)
        twelfth = (index * 5462) >> 16
        feature = (twelfth & 7) * 96 + (twelfth >> 3) * 24 + half * 12 + (index - 12 * twelfth)
        pick = one_hot(feature == iota((384, 768), 1))
        tg[half, :, 0:256] = nt(pick, tok_p).astype(BF16)
        tg[half, :, 256:512] = nt(pick, gy_p).astype(BF16)
    remote(tg.at[1 - core], ptg, cs_sem.at[0], cr_sem.at[0], {"seq": peer}).start()

    def arrived(ref, sem, spare):
        remote(ref, ref, spare, sem, {"seq": peer}).wait_recv()

    def left(ref, sem, spare):
        remote(ref, ref, sem, spare, {"seq": peer}).wait_send()

    for lv in range(3):
        for j in range(3):
            i = 3 * lv + j
            place = position[lv] + offset(lv, j)
            inside = (place >= 0) & (place < extent[lv])
            factor = jnp.where(inside, jnp.float32(2 << lv), jnp.float32(0.0))
            arrived(kvc.at[i], fr_sem.at[i], fs_sem.at[i])
            forward(kvc.at[i], kvtc.at[i], qmc.at[lv], wc.at[i], numc, denc, factor, 128)
    for j in (0, 2):
        arrived(kv0.at[j], fr_sem.at[9 + j // 2], fs_sem.at[9 + j // 2])
        forward(kv0.at[j], kvt0.at[j], qm0, w0.at[j], num0, den0, keep0(j), 256)

    lane = iota((1, 128), 1)
    gm0[...] = jnp.zeros(gm0.shape, BF16)
    gmc[...] = jnp.zeros(gmc.shape, BF16)
    for h in range(3):
        rows = slice(64 * h, 64 * h + 64)
        grows = slice(64 * h + 64, 64 * h + 128)
        coarse = jnp.sum(denc[:, 128 * h : 128 * h + 128], axis=0, keepdims=True)
        den = jnp.sum(den0[:, 256 * h : 256 * h + 256], axis=0, keepdims=True)
        inverse = 1.0 / (den + jnp.concatenate([coarse, coarse], axis=1))
        more = numc[rows, :]
        att = ((num0[rows, :] + jnp.concatenate([more, more], axis=1)) * inverse).astype(BF16)
        ra[192 + 64 * h : 256 + 64 * h, 256:512] = att
        att_s[rows, :] = att
        d_att = dot_s[rows, :].astype(F32)
        g = d_att * inverse
        c = jnp.sum(d_att * att.astype(F32), axis=0, keepdims=True) * inverse
        gm0[grows, 256 * h : 256 * h + 256] = g.astype(BF16)
        c0[:, 256 * h : 256 * h + 256] = jnp.broadcast_to(c, (8, 256))
        g = g[:, 0:128] + g[:, 128:256]
        c = c[:, 0:128] + c[:, 128:256]
        for lv in range(3):
            if lv > 0:
                g = g + pltpu.roll(g, 128 >> lv, 1)
                c = c + pltpu.roll(jnp.broadcast_to(c, (8, 128)), 128 >> lv, 1)[0:1]
            used = lane < (128 >> lv)
            gmc[lv, grows, 128 * h : 128 * h + 128] = jnp.where(used, g, 0.0).astype(BF16)
            cc[lv, :, 128 * h : 128 * h + 128] = jnp.broadcast_to(
                jnp.where(used, c, 0.0), (8, 128)
            )
    remote(
        ra.at[pl.ds(192, 192), pl.ds(256, 256)], pra.at[pl.ds(192, 192), pl.ds(256, 256)],
        cs_sem.at[1], cr_sem.at[1], {"seq": peer},
    ).start()

    def backward(keys, keyst, qm, gm, c_rows, w_ref, dq, n):
        count = keys.shape[0]
        dk = jnp.zeros((count, 256), F32)
        dv = jnp.zeros((count, 256), F32)
        for h in range(3):
            lanes = slice(h * n, h * n + n)
            wb = w_ref[:, lanes]
            inner = nn(keys[:, 128:384], gm[:, lanes])
            slope = (wb.astype(F32) * (inner - c_rows[0:1, lanes])).astype(BF16)
            dq[64 * h : 64 * h + 64, :] += nn(keyst[64 * h : 64 * h + 64, :], slope)
            dk += nt(slope, qm[:, lanes])
            dv += nt(wb, gm[:, lanes])
        return jnp.concatenate(
            [dk[:, 0:128], dk[:, 128:256] + dv[:, 0:128], dv[:, 128:256]], axis=1
        )

    for lv in (2, 1, 0):
        rows = 128 >> lv
        mine = lax.rem(s, 1 << lv) * rows
        for j in range(3):
            i = 3 * lv + j
            k = 3 * lv + back_slot(j)
            dsendc[i] = backward(
                kvc.at[i], kvtc.at[i], qmc.at[lv], gmc.at[lv], cc.at[lv], wc.at[i], dqc.at[lv], 128
            ).astype(BF16)
            for part in range(1 << lv):
                remote(
                    dsendc.at[i, pl.ds(part * rows, rows)],
                    retc.at[k, pl.ds(mine, rows)],
                    bs_sem.at[k], br_sem.at[k], {"seq": target(lv, j, part)},
                ).start()
    for j in (0, 2):
        dsend0[j // 2] = backward(
            kv0.at[j], kvt0.at[j], qm0, gm0, c0, w0.at[j], dq0, 256
        ).astype(BF16)
        k = 1 - j // 2
        remote(
            dsend0.at[j // 2], ret0.at[k], bs_sem.at[9 + k], br_sem.at[9 + k],
            {"seq": prev_dev if j == 0 else next_dev},
        ).start()
    down[...] = backward(kv0.at[1], kvt0.at[1], qm0, gm0, c0, w0.at[1], dq0, 256)

    def spread(grad, lv):
        if lv == 0:
            return jnp.concatenate([grad, grad], axis=1)
        return grad + pltpu.roll(grad, 128 >> lv, 1)

    grad = round_low(dqc[2] * 0.5)
    for lv in (2, 1, 0):
        grad = unit_back(uc[lv, 0:192, :], grad) * 0.5
        base = dqc[lv - 1] if lv > 0 else dq0[...]
        grad = round_low(base * 0.5) + spread(grad, lv)
    dq_t = unit_back(u0[0:192, :], grad).astype(BF16)
    ra[0:192, 0:256] = dq_t
    remote(
        ra.at[pl.ds(0, 192), pl.ds(0, 256)], pra.at[pl.ds(0, 192), pl.ds(0, 256)],
        cs_sem.at[2], cr_sem.at[2], {"seq": peer},
    ).start()

    def column_parts(left_rows, weight, emit):
        for j in range(4):
            emit(j, nn(left_rows, weight[:, WINDOWS[j] : WINDOWS[j] + 256]))

    def own_columns(j, total):
        if j % 2 == 1:
            total = pltpu.roll(total, 192, 1)
        return total[:, 0:192].astype(BF16)

    def emit_mixed(j, total):
        mixs[j] = own_columns(j, total)

    column_parts(nt(permt[...], att_s[...]).astype(BF16), wout_ref, emit_mixed)
    for k in range(1, 4):
        remote(
            mixs.at[mp_dev(k)], mixr.at[k - 1], ms_sem.at[k - 1], mr_sem.at[k - 1],
            {"mp": mp_dev(k)},
        ).start()

    def emit_first(j, total):
        gtacc[j] = total

    column_parts(nt(permt[...], dq_t).astype(BF16), wqkv_ref.at[pl.ds(0, 192)], emit_first)

    def y_stage(r, total):
        gf[r] = total
        gs[r] = total.astype(BF16)
        for k in range(1, 4):
            remote(
                gs.at[r, pl.ds(lax.rem(y + k, 4) * 96, 96)], yr.at[r, k - 1],
                ys_sem.at[3 * r + k - 1], yr_sem.at[3 * r + k - 1], {"seq": y_dev(k)},
            ).start()

    at16 = iota((128, 96), 0)
    widen = one_hot(
        ((at16 >> 4) * 12 + (at16 & 15) == iota((128, 96), 1)) & ((at16 & 15) < 12)
    )

    def z_stage(r):
        total = gf[r, pl.ds(y * 96, 96), :]
        for k in range(3):
            arrived(yr.at[r, k], yr_sem.at[3 * r + k], ys_sem.at[3 * r + k])
            total += yr[r, k].astype(F32)
        zs[r] = nn(widen, total.astype(BF16)).astype(BF16)
        for k in range(1, 8):
            remote(
                zs.at[r, pl.ds(lax.rem(z + k, 8) * 16, 16)], zr.at[r, k - 1],
                zs_sem.at[7 * r + k - 1], zr_sem.at[7 * r + k - 1], {"seq": z_dev(k)},
            ).start()

    def z_finish(r, out):
        total = zs[r, pl.ds(z * 16, 16), :].astype(F32)
        for k in range(7):
            arrived(zr.at[r, k], zr_sem.at[7 * r + k], zs_sem.at[7 * r + k])
            total += zr[r, k].astype(F32)
        out[...] = total * NORM

    arrived(ptg, cr_sem.at[0], cs_sem.at[0])
    arrived(pra.at[pl.ds(192, 192), pl.ds(256, 256)], cr_sem.at[1], cs_sem.at[1])
    arrived(pra.at[pl.ds(0, 192), pl.ds(0, 256)], cr_sem.at[2], cs_sem.at[2])
    y_stage(0, nt(tg[core], ra[...]) + nt(ptg[...], pra[...]))

    def received(lv):
        rows = 128 >> lv
        total = jnp.zeros((rows, 384), F32)
        for j in range(3):
            i = 3 * lv + j
            arrived(retc.at[i], br_sem.at[i], bs_sem.at[i])
            for part in range(1 << lv):
                total += retc[i, part * rows : part * rows + rows, :].astype(F32)
        total = round_low(total)
        if lv > 0:
            total = jnp.concatenate([total, jnp.zeros((128 - rows, 384), F32)], axis=0)
        return total.T

    total = received(2)
    for lv in (2, 1, 0):
        grad_k = unit_back(uc[lv, 192:384, :], total[0:192]) * 0.5
        grad_v = total[192:384] * ROOT_HALF
        if lv > 0:
            base = received(lv - 1)
        else:
            base = down[...]
            for j in range(2):
                arrived(ret0.at[j], br_sem.at[9 + j], bs_sem.at[9 + j])
                base += ret0[j].astype(F32)
            base = round_low(base).T
        total = base + jnp.concatenate([spread(grad_k, lv), spread(grad_v, lv)], axis=0)
    dkv = jnp.concatenate([unit_back(u0[192:384, :], total[0:192]), total[192:384]], axis=0)
    dkvt[...] = dkv.astype(BF16)
    remote(dkvt, pdkvt, cs_sem.at[3], cr_sem.at[3], {"seq": peer}).start()

    def emit_tokens(j, total):
        gts[j] = own_columns(j, total + gtacc[j])

    column_parts(nt(permt[...], dkvt[...]).astype(BF16), wqkv_ref.at[pl.ds(192, 384)], emit_tokens)
    for k in range(1, 4):
        remote(
            gts.at[mp_dev(k)], gtr.at[k - 1], ms_sem.at[2 + k], mr_sem.at[2 + k],
            {"mp": mp_dev(k)},
        ).start()
    z_stage(0)
    first = nt(tg[core, :, 0:256], dkvt[...])
    arrived(pdkvt, cr_sem.at[3], cs_sem.at[3])
    y_stage(1, first + nt(ptg[:, 0:256], pdkvt[...]))

    def mp_finish(sent, got, base, out):
        total = sent[m].astype(F32)
        for k in range(3):
            arrived(got.at[k], mr_sem.at[base + k], ms_sem.at[base + k])
            total += got[k].astype(F32)
        out[...] = total.astype(BF16)

    mp_finish(mixs, mixr, 0, mixed_ref)
    z_stage(1)
    mp_finish(gts, gtr, 3, gt_ref)
    z_finish(0, oa_ref)
    z_finish(1, ob_ref)

    for i in range(9):
        left(dsendc.at[i], fs_sem.at[i], fr_sem.at[i])
        left(dsendc.at[i], bs_sem.at[i], br_sem.at[i])
    for i in range(2):
        left(dsend0.at[i], fs_sem.at[9 + i], fr_sem.at[9 + i])
        left(dsend0.at[i], bs_sem.at[9 + i], br_sem.at[9 + i])
    left(ptg, cs_sem.at[0], cr_sem.at[0])
    left(ra.at[pl.ds(192, 192), pl.ds(256, 256)], cs_sem.at[1], cr_sem.at[1])
    left(ra.at[pl.ds(0, 192), pl.ds(0, 256)], cs_sem.at[2], cr_sem.at[2])
    left(dkvt, cs_sem.at[3], cr_sem.at[3])
    for i in range(6):
        left(mixs.at[0], ms_sem.at[i], mr_sem.at[i])
        left(gs.at[0, pl.ds(0, 96)], ys_sem.at[i], yr_sem.at[i])
    for i in range(14):
        left(zs.at[0, pl.ds(0, 16)], zs_sem.at[i], zr_sem.at[i])


def shards(tokens, w_qkv, w_out, grad_y):
    vmem = pl.BlockSpec(memory_space=pltpu.VMEM)
    low = lambda *shape: pltpu.VMEM(shape, BF16)
    wide = lambda *shape: pltpu.VMEM(shape, F32)
    sems = lambda count: pltpu.SemaphoreType.DMA((count,))
    scratch = [
        low(256, 256), wide(576, 256), wide(3, 384, 128),
        low(3, 256, 384), low(9, 128, 384), low(3, 128, 384), low(3, 384, 256), low(9, 384, 128),
        low(3, 256, 768), low(9, 128, 384), low(256, 768), low(3, 256, 384),
        low(256, 768), low(3, 256, 384), wide(8, 768), wide(3, 8, 384),
        wide(192, 256), wide(192, 128), wide(8, 768), wide(8, 384), low(192, 256), low(192, 256),
        wide(192, 256), wide(3, 192, 128), wide(256, 384),
        low(2, 256, 384), low(9, 128, 384), low(2, 256, 384), low(9, 128, 384),
        low(2, 384, 512), low(384, 512), low(384, 512), low(384, 512), low(384, 256), low(384, 256),
        low(4, 256, 192), low(3, 256, 192), wide(4, 256, 256), low(4, 256, 192), low(3, 256, 192),
        wide(2, 384, 384), low(2, 384, 384), low(2, 3, 96, 384), low(2, 128, 384),
        low(2, 7, 16, 384),
        sems(11), sems(11), sems(11), sems(11), sems(4), sems(4),
        sems(6), sems(6), sems(6), sems(6), sems(14), sems(14),
    ]
    mixed, grad_tokens, part_a, part_b = pl.pallas_call(
        kernel,
        out_shape=(
            jax.ShapeDtypeStruct((256, 192), BF16),
            jax.ShapeDtypeStruct((256, 192), BF16),
            jax.ShapeDtypeStruct((16, 384), F32),
            jax.ShapeDtypeStruct((16, 384), F32),
        ),
        in_specs=[vmem] * 4,
        out_specs=(vmem,) * 4,
        scratch_shapes=scratch,
        compiler_params=pltpu.CompilerParams(
            collective_id=0, has_side_effects=True, vmem_limit_bytes=48 * 1024 * 1024
        ),
        cost_estimate=pl.CostEstimate(
            flops=2_000_000_000, bytes_accessed=4_000_000, transcendentals=1_000_000
        ),
    )(
        tokens.reshape(256, 768), w_qkv.reshape(576, 768), w_out, grad_y.reshape(256, 768)
    )
    grad_wqkv = jnp.stack([part_a[:12, :192], part_b[:12, :192], part_b[:12, 192:]], axis=1)
    grad_wout = part_a[:12, 192:]
    return (mixed[None], grad_tokens[None], grad_wqkv, grad_wout)


def solution(mesh):
    in_specs = (P(None, "seq", None), P(None, "mp", None), P("mp", None), P(None, "seq", None))
    out_specs = (P(None, "seq", "mp"), P(None, "seq", "mp"), P("seq", None, "mp"), P("seq", "mp"))
    return jax.shard_map(shards, mesh=mesh, in_specs=in_specs, out_specs=out_specs, check_vma=False)
```

time: 447 us -> 69.4 us (0.16)
  waiting for transfers between devices: 201 us -> 0 us
  starting transfers between devices: 102 us -> 0 us
  local copies, waits for them, and re-layouts: 79.2 us -> 7 us
  Pallas kernels: 0 us -> 61.3 us
  other arithmetic: 26.5 us -> 0.01 us
  between operations: 19.3 us -> 0.65 us
  matrix products: 17.3 us -> 0 us
    unnamed x6 -> x0, waiting for transfers between devices: 193 us -> none
    ppermute x34 -> x0, starting transfers between devices: 102 us -> none  [the longest x26 91.3 us: shifted(): lax.ppermute(value, axis, [(source, source + steps) for source in range(l...]
    pallas_call x0 -> x1, Pallas kernels: none -> 61.3 us  [shards(): pl.pallas_call(kernel, out_shape=(jax.ShapeDtypeStruct((256, 192), BF16),...]
    broadcast_in_dim x62 -> x0, local copies, waits for them, and re-layouts: 27.2 us -> none  [the longest x25 13.1 us: shards(): denom = denom + jnp.repeat(denom_part[:, 0], 2 ** level_index, axis=1)]
    dot_general x30 -> x0, matrix products: 17.3 us -> none  [the longest x4 3.62 us: block_backward(): jnp.einsum('sqhij,sqjhe->sqihe', slopes, key_blocks, preferred_element_ty...]
    unnamed x292 -> x11, local copies, waits for them, and re-layouts: 19.6 us -> 6.25 us
    reduce_sum x27 -> x0, other arithmetic: 8.96 us -> none  [the longest x6 3.95 us: pool_total(): jnp.sum(values_in.reshape((extent[0], extent[1] // factor, factor) + exte...]
    reshape x12 -> x0, local copies, waits for them, and re-layouts: 8.62 us -> none  [the longest x7 4.71 us: shards(): denom = denom_part.reshape(seq_count, row_count, local_heads)]
  transfers between devices with their start and end apart: 37 -> 0, of which waited for: 7 -> 0; matrix products, arithmetic and copies ran while one was open for 18% -> 0% of each run, Pallas kernels for 0% -> 0%
where the time goes in v1:
time: 69.4 us; the launch traced here: 69 us
  Pallas kernels  61.3 us (88%)
  local copies, waits for them, and re-layouts  7 us (10%)
    pallas_call x1, Pallas kernels, shards(): pl.pallas_call(kernel, out_shape=(jax.ShapeDtypeStruct((256, 192), BF16),...  61.3 us
    unnamed x11, local copies, waits for them, and re-layouts  6.25 us

profile of v1, /device:TPU:2, one launch (start us, length us, event | category | flops | bytes accessed | tf_op | source)
XLA Modules:
  0.0 69.0 jit_solution(17593833149369485541)
XLA Ops:
  0.6 0.0 copy-start
  0.6 1.2 %copy-done = bf16[3,192,768]{2,1,0:T(8,128)(2,1)S(1)} copy-done((bf16[3,192,768]{2,1,0:T(8,128)(2,1)S(1)}, bf16[3,192,768]{2,1,0:T(8,128)(2,1)}, u32[]{:S(2)}) %copy-start) | copy-done | bytes 884760
  1.8 0.0 copy-start.1
  1.8 1.0 %copy-done.1 = bf16[1,256,768]{2,1,0:T(8,128)(2,1)S(1)} copy-done((bf16[1,256,768]{2,1,0:T(8,128)(2,1)S(1)}, bf16[1,256,768]{2,1,0:T(8,128)(2,1)}, u32[]{:S(2)}) %copy-start.1) | copy-done | bytes 393240
  2.8 0.0 copy-start.2
  2.8 1.0 %copy-done.2 = bf16[1,256,768]{2,1,0:T(8,128)(2,1)S(1)} copy-done((bf16[1,256,768]{2,1,0:T(8,128)(2,1)S(1)}, bf16[1,256,768]{2,1,0:T(8,128)(2,1)}, u32[]{:S(2)}) %copy-start.2) | copy-done | bytes 393240
  3.8 0.0 copy-start.3
  3.8 1.0 %copy-done.3 = bf16[192,768]{1,0:T(8,128)(2,1)S(1)} copy-done((bf16[192,768]{1,0:T(8,128)(2,1)S(1)}, bf16[192,768]{1,0:T(8,128)(2,1)}, u32[]{:S(2)}) %copy-start.3) | copy-done | bytes 294936
  4.8 61.3 %shard_map.75 = (bf16[256,192]{1,0:T(8,128)(2,1)S(1)}, bf16[256,192]{1,0:T(8,128)(2,1)S(1)}, f32[16,384]{1,0:T(8,128)S(1)}, f32[16,384]{1,0:T(8,128)S(1)}) custom-call(bf16[256,768]{1,0:T(8,128)(2,1)S(1)} %bitcast.14, bf16[576,768]{1,0:T(8,128)(2,1)S(1)} %bitcast.13, bf16[192,768]{1,0:T(8,128)(2,1)S(1)} %copy-done.3, bf16[256,768]{1,0:T(8,128)(2,1)S(1)} %bitcast.15), custom_call_target="tpu_custom_call" | custom-call | flops 2000000000 | bytes 4000000 | tf_op jit(solution)/shard_map/pallas_call | solution.py:471
  66.1 0.7 %copy.8 = bf16[1,256,192]{1,2,0:T(8,128)(2,1)} copy(bf16[1,256,192]{2,1,0:T(8,128)(2,1)S(1)} %bitcast.12) | data formatting | bytes 196608
  66.8 0.7 %copy.9 = bf16[1,256,192]{1,2,0:T(8,128)(2,1)} copy(bf16[1,256,192]{2,1,0:T(8,128)(2,1)S(1)} %bitcast.11) | data formatting | bytes 196608
  67.6 0.7 fusion
  68.2 0.1 slice_bitcast_fusion.1
  68.3 0.6 copy.10
  (1 shorter events, 0.0 us)
Async XLA Ops:
  0.6 1.2 %copy-start = (bf16[3,192,768]{2,1,0:T(8,128)(2,1)S(1)}, bf16[3,192,768]{2,1,0:T(8,128)(2,1)}, u32[]{:S(2)}) copy-start(bf16[3,192,768]{2,1,0:T(8,128)(2,1)} %param.5) | copy-start | bytes 2654212
  1.8 1.0 %copy-start.1 = (bf16[1,256,768]{2,1,0:T(8,128)(2,1)S(1)}, bf16[1,256,768]{2,1,0:T(8,128)(2,1)}, u32[]{:S(2)}) copy-start(bf16[1,256,768]{2,1,0:T(8,128)(2,1)} %param.4) | copy-start | bytes 1179652
  2.8 1.0 %copy-start.2 = (bf16[1,256,768]{2,1,0:T(8,128)(2,1)S(1)}, bf16[1,256,768]{2,1,0:T(8,128)(2,1)}, u32[]{:S(2)}) copy-start(bf16[1,256,768]{2,1,0:T(8,128)(2,1)} %param.7) | copy-start | bytes 1179652
  3.8 1.0 %copy-start.3 = (bf16[192,768]{1,0:T(8,128)(2,1)S(1)}, bf16[192,768]{1,0:T(8,128)(2,1)}, u32[]{:S(2)}) copy-start(bf16[192,768]{1,0:T(8,128)(2,1)} %wout_ref.1) | copy-start | bytes 884740

commit v2 on v1

--- a/solution.py
+++ b/solution.py
@@ -11,7 +11,6 @@
 EPS = 1e-06
 ROOT_HALF = 0.7071067811865476
 NORM = 1.0 / 128.0
-WINDOWS = (0, 128, 384, 512)
 
 
 def nn(a, b):
@@ -56,14 +55,30 @@
 
 
 def kernel(
-    tok_ref, wqkv_ref, wout_ref, gy_ref,
-    mixed_ref, gt_ref, oa_ref, ob_ref,
-    permt, u0, uc, kv0, kvc, ownc, kvt0, kvtc, w0, wc, qm0, qmc, gm0, gmc, c0, cc,
-    num0, numc, den0, denc, dot_s, att_s, dq0, dqc, down, dsend0, dsendc, ret0, retc,
+    tok_hbm, wqkv_hbm, wout_hbm, gy_hbm,
+    mixed_ref, gt_ref, gw_ref, go_ref,
+    tok_ref, wqkv_ref, wout_ref, gy_ref, wot, wqt, wkvt,
+    perm_s, u0, uc, kv0, kvc, ownc, kvt0, kvtc, w0, wc, qm0, qmc, gm0, gmc, c0, cc,
+    num0, numc, den0, denc, dot_s, att_s, dq0, dqc, down, dsend0, dsendc, ret0, ret1, retc,
+    own1, ownf, sib1, sibc, out1, outc,
     tg, ptg, ra, pra, dkvt, pdkvt, mixs, mixr, gtacc, gts, gtr,
     gf, gs, yr, zs, zr,
-    fs_sem, fr_sem, bs_sem, br_sem, cs_sem, cr_sem, ms_sem, mr_sem, ys_sem, yr_sem, zs_sem, zr_sem,
+    in_sem, fs_sem, fr_sem, hs_sem, hr_sem, bs_sem, br_sem, ss_sem, sr_sem,
+    cs_sem, cr_sem, ms_sem, mr_sem, ys_sem, yr_sem, zs_sem, zr_sem,
 ):
+    loads = [
+        pltpu.make_async_copy(src, dst, in_sem.at[n])
+        for n, (src, dst) in enumerate((
+            (tok_hbm, tok_ref),
+            (wqkv_hbm.at[pl.ds(192, 384)], wqkv_ref.at[pl.ds(192, 384)]),
+            (wqkv_hbm.at[pl.ds(0, 192)], wqkv_ref.at[pl.ds(0, 192)]),
+            (gy_hbm, gy_ref),
+            (wout_hbm, wout_ref),
+        ))
+    ]
+    for load in loads:
+        load.start()
+
     s = lax.axis_index("seq")
     m = lax.axis_index("mp")
     core = lax.rem(s, 2)
@@ -78,7 +93,10 @@
 
     def target(lv, j, part):
         block = lax.rem(position[lv] + offset(lv, j) + extent[lv], extent[lv])
-        return block * (1 << lv) + part
+        return block if lv == 0 else block * (1 << lv) + 2 * part + core
+
+    def parts(lv):
+        return 2 if lv == 2 else 1
 
     def back_slot(j):
         return (1, 0, 2)[j]
@@ -99,13 +117,12 @@
     barrier = pltpu.get_barrier_semaphore()
     partners = [{"seq": prev_dev}, {"seq": next_dev}]
     for lv in range(3):
-        for j in range(3):
-            for part in range(1 << lv):
+        for j in range(2 if lv == 0 else 3):
+            for part in range(parts(lv)):
                 partners.append({"seq": target(lv, j, part)})
     partners += [{"seq": y_dev(k)} for k in range(1, 4)]
     partners += [{"seq": z_dev(k)} for k in range(1, 8)]
     partners += [{"mp": mp_dev(k)} for k in range(1, 4)]
-    partners += [{"seq": peer}]
     for partner in partners:
         pl.semaphore_signal(barrier, inc=1, device_id=partner, device_id_type=MESH)
 
@@ -115,12 +132,47 @@
             device_id=where, device_id_type=MESH,
         )
 
-    row = iota((256, 256), 0)
-    col = iota((256, 256), 1)
-    perm = one_hot(natural_token(row) == col)
-    permt[...] = one_hot(natural_token(col) == row)
+    def arrived(ref, sem, spare):
+        remote(ref, ref, spare, sem, {"seq": peer}).wait_recv()
+
+    def left(ref, sem, spare):
+        remote(ref, ref, sem, spare, {"seq": peer}).wait_send()
+
+    perm = one_hot(natural_token(iota((256, 256), 0)) == iota((256, 256), 1))
+    perm_s[...] = perm
+    loads[0].wait()
     tok_p = nn(perm, tok_ref[...]).astype(BF16)
-    u0[...] = nt(wqkv_ref[...], tok_p)
+    loads[1].wait()
+    u0[192:576, :] = nt(wqkv_ref[192:576, :], tok_p)
+
+    def halves(x, lv):
+        return x[:, 0:128] + x[:, 128:256] if lv == 0 else x + pltpu.roll(x, 128 >> lv, 1)
+
+    key = unit(u0[192:384, :])
+    v = u0[384:576, :]
+    kv0[1] = jnp.concatenate([key, v], axis=0).T.astype(BF16)
+    for lv in range(3):
+        mean = halves(key, lv) * 0.5
+        v = halves(v, lv) * ROOT_HALF
+        uc[lv, 192:384, :] = mean
+        key = unit(mean)
+        ownc[lv] = jnp.concatenate([key, v], axis=0).T.astype(BF16)
+
+    pl.semaphore_wait(barrier, len(partners))
+
+    mine = (0, core * 64, core * 64 + lax.rem(s // 2, 2) * 32)
+    for lv in range(3):
+        rows = 128 >> lv
+        for j in range(2 if lv == 0 else 3):
+            i = 3 * lv + back_slot(j)
+            for part in range(parts(lv)):
+                remote(
+                    ownc.at[lv, pl.ds(0, rows)],
+                    kvc.at[i, pl.ds(mine[lv], rows)],
+                    fs_sem.at[i], fr_sem.at[i], {"seq": target(lv, j, part)},
+                ).start()
+    remote(kv0.at[1], kv0.at[0], fs_sem.at[9], fr_sem.at[9], {"seq": next_dev}).start()
+    remote(kv0.at[1], kv0.at[2], fs_sem.at[10], fr_sem.at[10], {"seq": prev_dev}).start()
 
     def store_q(dst, q_rows, n):
         dst[...] = jnp.zeros(dst.shape, BF16)
@@ -128,37 +180,15 @@
         for h in range(3):
             dst[64 * h : 64 * h + 64, h * n : h * n + n] = half[64 * h : 64 * h + 64]
 
-    qk = unit(u0[0:384, :])
-    v = u0[384:576, :]
-    store_q(qm0, qk[0:192], 256)
-    kv0[1] = jnp.concatenate([qk[192:384], v], axis=0).T.astype(BF16)
+    loads[2].wait()
+    u0[0:192, :] = nt(wqkv_ref[0:192, :], tok_p)
+    query = unit(u0[0:192, :])
+    store_q(qm0, query, 256)
     for lv in range(3):
-        if lv == 0:
-            mean = (qk[:, 0:128] + qk[:, 128:256]) * 0.5
-            v = (v[:, 0:128] + v[:, 128:256]) * ROOT_HALF
-        else:
-            mean = (qk + pltpu.roll(qk, 128 >> lv, 1)) * 0.5
-            v = (v + pltpu.roll(v, 128 >> lv, 1)) * ROOT_HALF
-        uc[lv] = mean
-        qk = unit(mean)
-        store_q(qmc.at[lv], qk[0:192], 128)
-        ownc[lv] = jnp.concatenate([qk[192:384], v], axis=0).T.astype(BF16)
-
-    pl.semaphore_wait(barrier, len(partners))
-
-    for lv in range(3):
-        rows = 128 >> lv
-        mine = lax.rem(s, 1 << lv) * rows
-        for j in range(3):
-            i = 3 * lv + back_slot(j)
-            for part in range(1 << lv):
-                remote(
-                    ownc.at[lv, pl.ds(0, rows)],
-                    kvc.at[i, pl.ds(mine, rows)],
-                    fs_sem.at[i], fr_sem.at[i], {"seq": target(lv, j, part)},
-                ).start()
-    remote(kv0.at[1], kv0.at[0], fs_sem.at[9], fr_sem.at[9], {"seq": next_dev}).start()
-    remote(kv0.at[1], kv0.at[2], fs_sem.at[10], fr_sem.at[10], {"seq": prev_dev}).start()
+        mean = halves(query, lv) * 0.5
+        uc[lv, 0:192, :] = mean
+        query = unit(mean)
+        store_q(qmc.at[lv], query, 128)
 
     num0[...] = jnp.zeros(num0.shape, F32)
     numc[...] = jnp.zeros(numc.shape, F32)
@@ -190,6 +220,8 @@
 
     forward(kv0.at[1], kvt0.at[1], qm0, w0.at[1], num0, den0, keep0(1), 256)
 
+    loads[3].wait()
+    loads[4].wait()
     gy_p = nn(perm, gy_ref[...]).astype(BF16)
     dot_s[...] = nt(wout_ref[...], gy_p).astype(BF16)
     for half in range(2):
@@ -201,23 +233,40 @@
         tg[half, :, 256:512] = nt(pick, gy_p).astype(BF16)
     remote(tg.at[1 - core], ptg, cs_sem.at[0], cr_sem.at[0], {"seq": peer}).start()
 
-    def arrived(ref, sem, spare):
-        remote(ref, ref, spare, sem, {"seq": peer}).wait_recv()
-
-    def left(ref, sem, spare):
-        remote(ref, ref, sem, spare, {"seq": peer}).wait_send()
-
-    for lv in range(3):
-        for j in range(3):
-            i = 3 * lv + j
-            place = position[lv] + offset(lv, j)
-            inside = (place >= 0) & (place < extent[lv])
-            factor = jnp.where(inside, jnp.float32(2 << lv), jnp.float32(0.0))
-            arrived(kvc.at[i], fr_sem.at[i], fs_sem.at[i])
-            forward(kvc.at[i], kvtc.at[i], qmc.at[lv], wc.at[i], numc, denc, factor, 128)
+    same = one_hot(iota((256, 256), 0) == iota((256, 256), 1))
+    for n in range(3):
+        cut = slice(256 * n, 256 * n + 256)
+        wot[cut, :] = nt(same, wout_ref[:, cut]).astype(BF16)
+        wqt[cut, :] = nt(same, wqkv_ref[0:192, cut]).astype(BF16)
+        wkvt[cut, :] = nt(same, wqkv_ref[192:576, cut]).astype(BF16)
+
+    half = core * 64
+    other = 64 - half
+    arrived(kvc.at[0], fr_sem.at[0], fs_sem.at[0])
+    arrived(kvc.at[1], fr_sem.at[1], fs_sem.at[1])
+    remote(kvc.at[core], kvc.at[2], hs_sem.at[2], hr_sem.at[2], {"seq": peer}).start()
+    for i in range(3, 9):
+        piece = kvc.at[i, pl.ds(half, 64)]
+        arrived(piece, fr_sem.at[i], fs_sem.at[i])
+        remote(piece, piece, hs_sem.at[i], hr_sem.at[i], {"seq": peer}).start()
+
+    def coarse_forward(lv, j):
+        i = 3 * lv + j
+        place = position[lv] + offset(lv, j)
+        inside = (place >= 0) & (place < extent[lv])
+        factor = jnp.where(inside, jnp.float32(2 << lv), jnp.float32(0.0))
+        forward(kvc.at[i], kvtc.at[i], qmc.at[lv], wc.at[i], numc, denc, factor, 128)
+
+    coarse_forward(0, 0)
+    coarse_forward(0, 1)
     for j in (0, 2):
         arrived(kv0.at[j], fr_sem.at[9 + j // 2], fs_sem.at[9 + j // 2])
         forward(kv0.at[j], kvt0.at[j], qm0, w0.at[j], num0, den0, keep0(j), 256)
+    arrived(kvc.at[2], hr_sem.at[2], hs_sem.at[2])
+    coarse_forward(0, 2)
+    for i in range(3, 9):
+        arrived(kvc.at[i, pl.ds(other, 64)], hr_sem.at[i], hs_sem.at[i])
+        coarse_forward(i // 3, i % 3)
 
     lane = iota((1, 128), 1)
     gm0[...] = jnp.zeros(gm0.shape, BF16)
@@ -269,22 +318,42 @@
             [dk[:, 0:128], dk[:, 128:256] + dv[:, 0:128], dv[:, 128:256]], axis=1
         )
 
-    for lv in (2, 1, 0):
+    def coarse_backward(lv, i):
+        return backward(
+            kvc.at[i], kvtc.at[i], qmc.at[lv], gmc.at[lv], cc.at[lv], wc.at[i], dqc.at[lv], 128
+        )
+
+    def to_peer(i):
+        ownf[i - 3] = coarse_backward(i // 3, i)
+        dsendc[i - 3] = ownf[i - 3, pl.ds(other, 64), :].astype(BF16)
+        remote(
+            dsendc.at[i - 3], sibc.at[i - 3], ss_sem.at[i], sr_sem.at[i], {"seq": peer}
+        ).start()
+
+    def return_pair(i):
+        lv, j = i // 3, i % 3
+        arrived(sibc.at[i - 3], sr_sem.at[i], ss_sem.at[i])
+        outc[i - 3] = (
+            ownf[i - 3, pl.ds(half, 64), :] + sibc[i - 3].astype(F32)
+        ).astype(BF16)
+        k = 3 * lv + back_slot(j)
         rows = 128 >> lv
-        mine = lax.rem(s, 1 << lv) * rows
-        for j in range(3):
-            i = 3 * lv + j
-            k = 3 * lv + back_slot(j)
-            dsendc[i] = backward(
-                kvc.at[i], kvtc.at[i], qmc.at[lv], gmc.at[lv], cc.at[lv], wc.at[i], dqc.at[lv], 128
-            ).astype(BF16)
-            for part in range(1 << lv):
-                remote(
-                    dsendc.at[i, pl.ds(part * rows, rows)],
-                    retc.at[k, pl.ds(mine, rows)],
-                    bs_sem.at[k], br_sem.at[k], {"seq": target(lv, j, part)},
-                ).start()
-    for j in (0, 2):
+        into = 0 if lv == 1 else lax.rem(s // 2, 2) * 32
+        for part in range(parts(lv)):
+            remote(
+                outc.at[i - 3, pl.ds(part * rows, rows)], retc.at[k - 3, pl.ds(into, rows)],
+                bs_sem.at[k], br_sem.at[k], {"seq": target(lv, j, part)},
+            ).start()
+
+    def return_first(slot, value):
+        out1[slot] = value.astype(BF16)
+        where = lax.rem(s + 4 * slot - 2 + 64, 64)
+        remote(
+            out1.at[slot], ret1.at[1 - slot], bs_sem.at[1 - slot], br_sem.at[1 - slot],
+            {"seq": where},
+        ).start()
+
+    def near_backward(j):
         dsend0[j // 2] = backward(
             kv0.at[j], kvt0.at[j], qm0, gm0, c0, w0.at[j], dq0, 256
         ).astype(BF16)
@@ -293,6 +362,23 @@
             dsend0.at[j // 2], ret0.at[k], bs_sem.at[9 + k], br_sem.at[9 + k],
             {"seq": prev_dev if j == 0 else next_dev},
         ).start()
+
+    for i in range(6, 9):
+        to_peer(i)
+    for i in range(3, 6):
+        to_peer(i)
+    own1[...] = coarse_backward(0, 2).astype(BF16)
+    remote(own1, sib1, ss_sem.at[2], sr_sem.at[2], {"seq": peer}).start()
+    return_first(1 - core, coarse_backward(0, 1 - core))
+    for i in range(6, 9):
+        return_pair(i)
+    shared = coarse_backward(0, core)
+    for i in range(3, 6):
+        return_pair(i)
+    arrived(sib1, sr_sem.at[2], ss_sem.at[2])
+    return_first(core, shared + sib1[...].astype(F32))
+    near_backward(0)
+    near_backward(2)
     down[...] = backward(kv0.at[1], kvt0.at[1], qm0, gm0, c0, w0.at[1], dq0, 256)
 
     def spread(grad, lv):
@@ -312,29 +398,16 @@
         cs_sem.at[2], cr_sem.at[2], {"seq": peer},
     ).start()
 
-    def column_parts(left_rows, weight, emit):
-        for j in range(4):
-            emit(j, nn(left_rows, weight[:, WINDOWS[j] : WINDOWS[j] + 256]))
-
-    def own_columns(j, total):
-        if j % 2 == 1:
-            total = pltpu.roll(total, 192, 1)
-        return total[:, 0:192].astype(BF16)
-
-    def emit_mixed(j, total):
-        mixs[j] = own_columns(j, total)
-
-    column_parts(nt(permt[...], att_s[...]).astype(BF16), wout_ref, emit_mixed)
+    att_t = att_s[...]
+    for j in range(4):
+        mixs[j] = nn(wot[192 * j : 192 * j + 192, :], att_t).astype(BF16)
     for k in range(1, 4):
         remote(
             mixs.at[mp_dev(k)], mixr.at[k - 1], ms_sem.at[k - 1], mr_sem.at[k - 1],
             {"mp": mp_dev(k)},
         ).start()
-
-    def emit_first(j, total):
-        gtacc[j] = total
-
-    column_parts(nt(permt[...], dq_t).astype(BF16), wqkv_ref.at[pl.ds(0, 192)], emit_first)
+    for j in range(4):
+        gtacc[j] = nn(wqt[192 * j : 192 * j + 192, :], dq_t)
 
     def y_stage(r, total):
         gf[r] = total
@@ -362,12 +435,12 @@
                 zs_sem.at[7 * r + k - 1], zr_sem.at[7 * r + k - 1], {"seq": z_dev(k)},
             ).start()
 
-    def z_finish(r, out):
+    def z_finish(r):
         total = zs[r, pl.ds(z * 16, 16), :].astype(F32)
         for k in range(7):
             arrived(zr.at[r, k], zr_sem.at[7 * r + k], zs_sem.at[7 * r + k])
             total += zr[r, k].astype(F32)
-        out[...] = total * NORM
+        return total * NORM
 
     arrived(ptg, cr_sem.at[0], cs_sem.at[0])
     arrived(pra.at[pl.ds(192, 192), pl.ds(256, 256)], cr_sem.at[1], cs_sem.at[1])
@@ -375,15 +448,21 @@
     y_stage(0, nt(tg[core], ra[...]) + nt(ptg[...], pra[...]))
 
     def received(lv):
-        rows = 128 >> lv
-        total = jnp.zeros((rows, 384), F32)
-        for j in range(3):
-            i = 3 * lv + j
-            arrived(retc.at[i], br_sem.at[i], bs_sem.at[i])
-            for part in range(1 << lv):
-                total += retc[i, part * rows : part * rows + rows, :].astype(F32)
+        if lv == 0:
+            total = jnp.zeros((128, 384), F32)
+            for i in range(2):
+                arrived(ret1.at[i], br_sem.at[i], bs_sem.at[i])
+                total += ret1[i].astype(F32)
+        else:
+            total = jnp.zeros((64, 384), F32)
+            for i in range(3 * lv, 3 * lv + 3):
+                arrived(retc.at[i - 3], br_sem.at[i], bs_sem.at[i])
+                total += retc[i - 3].astype(F32)
+            if lv == 2:
+                total = total[0:32] + total[32:64]
         total = round_low(total)
         if lv > 0:
+            rows = 128 >> lv
             total = jnp.concatenate([total, jnp.zeros((128 - rows, 384), F32)], axis=0)
         return total.T
 
@@ -404,10 +483,9 @@
     dkvt[...] = dkv.astype(BF16)
     remote(dkvt, pdkvt, cs_sem.at[3], cr_sem.at[3], {"seq": peer}).start()
 
-    def emit_tokens(j, total):
-        gts[j] = own_columns(j, total + gtacc[j])
-
-    column_parts(nt(permt[...], dkvt[...]).astype(BF16), wqkv_ref.at[pl.ds(192, 384)], emit_tokens)
+    dkv_t = dkvt[...]
+    for j in range(4):
+        gts[j] = (nn(wkvt[192 * j : 192 * j + 192, :], dkv_t) + gtacc[j]).astype(BF16)
     for k in range(1, 4):
         remote(
             gts.at[mp_dev(k)], gtr.at[k - 1], ms_sem.at[2 + k], mr_sem.at[2 + k],
@@ -423,20 +501,30 @@
         for k in range(3):
             arrived(got.at[k], mr_sem.at[base + k], ms_sem.at[base + k])
             total += got[k].astype(F32)
-        out[...] = total.astype(BF16)
+        out[...] = nn(total.astype(BF16), perm_s[...]).astype(BF16)
 
     mp_finish(mixs, mixr, 0, mixed_ref)
     z_stage(1)
     mp_finish(gts, gtr, 3, gt_ref)
-    z_finish(0, oa_ref)
-    z_finish(1, ob_ref)
-
-    for i in range(9):
-        left(dsendc.at[i], fs_sem.at[i], fr_sem.at[i])
-        left(dsendc.at[i], bs_sem.at[i], br_sem.at[i])
+    first = z_finish(0)
+    go_ref[...] = pltpu.roll(first, 192, 1)[0:12, 0:192]
+    gw_ref[:, 0, :] = first[0:12, 0:192]
+    second = z_finish(1)
+    gw_ref[:, 1, :] = second[0:12, 0:192]
+    gw_ref[:, 2, :] = pltpu.roll(second, 192, 1)[0:12, 0:192]
+
     for i in range(2):
+        left(out1.at[i], fs_sem.at[i], fr_sem.at[i])
+        left(out1.at[i], bs_sem.at[i], br_sem.at[i])
         left(dsend0.at[i], fs_sem.at[9 + i], fr_sem.at[9 + i])
         left(dsend0.at[i], bs_sem.at[9 + i], br_sem.at[9 + i])
+    left(own1, hs_sem.at[2], hr_sem.at[2])
+    left(own1, ss_sem.at[2], sr_sem.at[2])
+    for i in range(3, 9):
+        left(outc.at[i - 3], fs_sem.at[i], fr_sem.at[i])
+        left(outc.at[i - 3], hs_sem.at[i], hr_sem.at[i])
+        left(outc.at[i - 3], ss_sem.at[i], sr_sem.at[i])
+        left(outc.at[i - 3], bs_sem.at[i], br_sem.at[i])
     left(ptg, cs_sem.at[0], cr_sem.at[0])
     left(ra.at[pl.ds(192, 192), pl.ds(256, 256)], cs_sem.at[1], cr_sem.at[1])
     left(ra.at[pl.ds(0, 192), pl.ds(0, 256)], cs_sem.at[2], cr_sem.at[2])
@@ -448,39 +536,56 @@
         left(zs.at[0, pl.ds(0, 16)], zs_sem.at[i], zr_sem.at[i])
 
 
+def deliver(*refs):
+    count = (len(refs) - 1) // 2
+    copies = [
+        pltpu.make_async_copy(refs[n], refs[count + n], refs[-1].at[n]) for n in range(count)
+    ]
+    for copy in copies:
+        copy.start()
+    for copy in copies:
+        copy.wait()
+
+
 def shards(tokens, w_qkv, w_out, grad_y):
     vmem = pl.BlockSpec(memory_space=pltpu.VMEM)
+    hbm = pl.BlockSpec(memory_space=pltpu.HBM)
     low = lambda *shape: pltpu.VMEM(shape, BF16)
     wide = lambda *shape: pltpu.VMEM(shape, F32)
     sems = lambda count: pltpu.SemaphoreType.DMA((count,))
     scratch = [
+        low(256, 768), low(576, 768), low(192, 768), low(256, 768),
+        low(768, 192), low(768, 192), low(768, 384),
         low(256, 256), wide(576, 256), wide(3, 384, 128),
         low(3, 256, 384), low(9, 128, 384), low(3, 128, 384), low(3, 384, 256), low(9, 384, 128),
         low(3, 256, 768), low(9, 128, 384), low(256, 768), low(3, 256, 384),
         low(256, 768), low(3, 256, 384), wide(8, 768), wide(3, 8, 384),
         wide(192, 256), wide(192, 128), wide(8, 768), wide(8, 384), low(192, 256), low(192, 256),
         wide(192, 256), wide(3, 192, 128), wide(256, 384),
-        low(2, 256, 384), low(9, 128, 384), low(2, 256, 384), low(9, 128, 384),
+        low(2, 256, 384), low(6, 64, 384), low(2, 256, 384), low(2, 128, 384), low(6, 64, 384),
+        low(128, 384), wide(6, 128, 384), low(128, 384), low(6, 64, 384),
+        low(2, 128, 384), low(6, 64, 384),
         low(2, 384, 512), low(384, 512), low(384, 512), low(384, 512), low(384, 256), low(384, 256),
-        low(4, 256, 192), low(3, 256, 192), wide(4, 256, 256), low(4, 256, 192), low(3, 256, 192),
+        low(4, 192, 256), low(3, 192, 256), wide(4, 192, 256), low(4, 192, 256), low(3, 192, 256),
         wide(2, 384, 384), low(2, 384, 384), low(2, 3, 96, 384), low(2, 128, 384),
         low(2, 7, 16, 384),
-        sems(11), sems(11), sems(11), sems(11), sems(4), sems(4),
-        sems(6), sems(6), sems(6), sems(6), sems(14), sems(14),
+        sems(5), sems(11), sems(11), sems(9), sems(9), sems(11), sems(11), sems(9), sems(9),
+        sems(4), sems(4), sems(6), sems(6), sems(6), sems(6), sems(14), sems(14),
     ]
-    mixed, grad_tokens, part_a, part_b = pl.pallas_call(
+    shapes = (
+        jax.ShapeDtypeStruct((192, 256), BF16),
+        jax.ShapeDtypeStruct((192, 256), BF16),
+        jax.ShapeDtypeStruct((12, 3, 192), F32),
+        jax.ShapeDtypeStruct((12, 192), F32),
+    )
+    results = pl.pallas_call(
         kernel,
-        out_shape=(
-            jax.ShapeDtypeStruct((256, 192), BF16),
-            jax.ShapeDtypeStruct((256, 192), BF16),
-            jax.ShapeDtypeStruct((16, 384), F32),
-            jax.ShapeDtypeStruct((16, 384), F32),
-        ),
-        in_specs=[vmem] * 4,
+        out_shape=shapes,
+        in_specs=[hbm] * 4,
         out_specs=(vmem,) * 4,
         scratch_shapes=scratch,
         compiler_params=pltpu.CompilerParams(
-            collective_id=0, has_side_effects=True, vmem_limit_bytes=48 * 1024 * 1024
+            collective_id=0, has_side_effects=True, vmem_limit_bytes=56098816
         ),
         cost_estimate=pl.CostEstimate(
             flops=2_000_000_000, bytes_accessed=4_000_000, transcendentals=1_000_000
@@ -488,9 +593,14 @@
     )(
         tokens.reshape(256, 768), w_qkv.reshape(576, 768), w_out, grad_y.reshape(256, 768)
     )
-    grad_wqkv = jnp.stack([part_a[:12, :192], part_b[:12, :192], part_b[:12, 192:]], axis=1)
-    grad_wout = part_a[:12, 192:]
-    return (mixed[None], grad_tokens[None], grad_wqkv, grad_wout)
+    mixed, grad_tokens, grad_wqkv, grad_wout = pl.pallas_call(
+        deliver,
+        out_shape=shapes,
+        in_specs=[vmem] * 4,
+        out_specs=(hbm,) * 4,
+        scratch_shapes=[sems(4)],
+    )(*results)
+    return (mixed.T[None], grad_tokens.T[None], grad_wqkv, grad_wout)
 
 
 def solution(mesh):

time: 69.4 us -> 60.4 us (0.87)
  Pallas kernels: 61.3 us -> 56.5 us
  local copies, waits for them, and re-layouts: 7 us -> 2.47 us
    pallas_call x1 -> x2, Pallas kernels: 61.3 us -> 56.5 us  [the longest x1 54.8 us: shards(): pl.pallas_call(kernel, out_shape=shapes, in_specs=[hbm] * 4, out_specs=(v...]
    unnamed x11 -> x8, local copies, waits for them, and re-layouts: 6.25 us -> 2.47 us
where the time goes in v2:
time: 60.4 us; the launch traced here: 59.6 us
  Pallas kernels  56.5 us (94%)
  local copies, waits for them, and re-layouts  2.47 us (4%)
  between operations  0.65 us (1%)
    pallas_call x1, Pallas kernels, shards(): pl.pallas_call(kernel, out_shape=shapes, in_specs=[hbm] * 4, out_specs=(v...  54.8 us
    unnamed x8, local copies, waits for them, and re-layouts  2.47 us
    pallas_call x1, Pallas kernels, shards(): pl.pallas_call(deliver, out_shape=shapes, in_specs=[vmem] * 4, out_specs=...  1.66 us

profile of v2, /device:TPU:2, one launch (start us, length us, event | category | flops | bytes accessed | tf_op | source)
XLA Modules:
  0.0 59.6 jit_solution(12915903026762255270)
XLA Ops:
  0.6 54.8 %shard_map.75 = (bf16[192,256]{1,0:T(8,128)(2,1)S(1)}, bf16[192,256]{1,0:T(8,128)(2,1)S(1)}, f32[12,3,192]{2,1,0:T(4,128)S(1)}, f32[12,192]{1,0:T(8,128)S(1)}) custom-call(bf16[256,768]{1,0:T(8,128)(2,1)} %bitcast.10, bf16[576,768]{1,0:T(8,128)(2,1)} %bitcast.9, bf16[192,768]{1,0:T(8,128)(2,1)} %wout_hbm.1, bf16[256,768]{1,0:T(8,128)(2,1)} %bitcast.11), custom_call_target="tpu_custom_call" | custom-call | flops 2000000000 | bytes 4000000 | tf_op jit(solution)/shard_map/pallas_call | solution.py:581
  55.4 0.0 copy-start
  55.5 0.6 %copy-done = bf16[192,256]{1,0:T(8,128)(2,1)} copy-done((bf16[192,256]{1,0:T(8,128)(2,1)}, bf16[192,256]{1,0:T(8,128)(2,1)S(1)}, u32[]{:S(2)}) %copy-start) | copy-done | bytes 98328
  56.1 0.0 copy-start.1
  56.1 0.6 %copy-done.1 = bf16[192,256]{1,0:T(8,128)(2,1)} copy-done((bf16[192,256]{1,0:T(8,128)(2,1)}, bf16[192,256]{1,0:T(8,128)(2,1)S(1)}, u32[]{:S(2)}) %copy-start.1) | copy-done | bytes 98328
  56.7 0.0 copy-start.2
  56.7 0.6 %copy-done.2 = f32[12,3,192]{2,1,0:T(4,128)} copy-done((f32[12,3,192]{2,1,0:T(4,128)}, f32[12,3,192]{2,1,0:T(4,128)S(1)}, u32[]{:S(2)}) %copy-start.2) | copy-done | bytes 27672
  57.3 0.0 copy-start.3
  57.3 0.6 copy-done.3
  57.9 1.7 %shard_map.76 = (bf16[192,256]{1,0:T(8,128)(2,1)}, bf16[192,256]{1,0:T(8,128)(2,1)}, f32[12,3,192]{2,1,0:T(4,128)}, f32[12,192]{1,0:T(8,128)}) custom-call(bf16[192,256]{1,0:T(8,128)(2,1)} %copy-done, bf16[192,256]{1,0:T(8,128)(2,1)} %copy-done.1, f32[12,3,192]{2,1,0:T(4,128)} %copy-done.2, f32[12,192]{1,0:T(8,128)} %copy-done.3), custom_call_target="tpu_custom_call" | custom-call | tf_op jit(solution)/shard_map/pallas_call | solution.py:596
Async XLA Ops:
  55.4 0.6 %copy-start = (bf16[192,256]{1,0:T(8,128)(2,1)}, bf16[192,256]{1,0:T(8,128)(2,1)S(1)}, u32[]{:S(2)}) copy-start(bf16[192,256]{1,0:T(8,128)(2,1)S(1)} %get-tuple-element.12.refs_0_) | copy-start | bytes 294916
  56.1 0.6 %copy-start.1 = (bf16[192,256]{1,0:T(8,128)(2,1)}, bf16[192,256]{1,0:T(8,128)(2,1)S(1)}, u32[]{:S(2)}) copy-start(bf16[192,256]{1,0:T(8,128)(2,1)S(1)} %get-tuple-element.13.refs_1_) | copy-start | bytes 294916
  56.7 0.6 %copy-start.2 = (f32[12,3,192]{2,1,0:T(4,128)}, f32[12,3,192]{2,1,0:T(4,128)S(1)}, u32[]{:S(2)}) copy-start(f32[12,3,192]{2,1,0:T(4,128)S(1)} %get-tuple-element.14.refs_2_) | copy-start | bytes 82948
  57.3 0.6 %copy-start.3 = (f32[12,192]{1,0:T(8,128)}, f32[12,192]{1,0:T(8,128)S(1)}, u32[]{:S(2)}) copy-start(f32[12,192]{1,0:T(8,128)S(1)} %get-tuple-element.15.refs_3_) | copy-start | bytes 27652

commit v3 on v2

--- a/solution.py
+++ b/solution.py
@@ -62,7 +62,7 @@
     num0, numc, den0, denc, dot_s, att_s, dq0, dqc, down, dsend0, dsendc, ret0, ret1, retc,
     own1, ownf, sib1, sibc, out1, outc,
     tg, ptg, ra, pra, dkvt, pdkvt, mixs, mixr, gtacc, gts, gtr,
-    gf, gs, yr, zs, zr,
+    gf, gs, zra, yra, yrb, zrb, wsa, wsb,
     in_sem, fs_sem, fr_sem, hs_sem, hr_sem, bs_sem, br_sem, ss_sem, sr_sem,
     cs_sem, cr_sem, ms_sem, mr_sem, ys_sem, yr_sem, zs_sem, zr_sem,
 ):
@@ -104,6 +104,7 @@
     prev_dev = lax.rem(s + 63, 64)
     next_dev = lax.rem(s + 1, 64)
     peer = s + 1 - 2 * core
+    across = lax.rem(s + 2 * core + 63, 64)
 
     def y_dev(k):
         return z * 8 + lax.rem(y + k, 4) * 2 + core
@@ -161,7 +162,7 @@
     pl.semaphore_wait(barrier, len(partners))
 
     mine = (0, core * 64, core * 64 + lax.rem(s // 2, 2) * 32)
-    for lv in range(3):
+    for lv in (2, 1, 0):
         rows = 128 >> lv
         for j in range(2 if lv == 0 else 3):
             i = 3 * lv + back_slot(j)
@@ -171,8 +172,8 @@
                     kvc.at[i, pl.ds(mine[lv], rows)],
                     fs_sem.at[i], fr_sem.at[i], {"seq": target(lv, j, part)},
                 ).start()
-    remote(kv0.at[1], kv0.at[0], fs_sem.at[9], fr_sem.at[9], {"seq": next_dev}).start()
-    remote(kv0.at[1], kv0.at[2], fs_sem.at[10], fr_sem.at[10], {"seq": prev_dev}).start()
+    remote(kv0.at[1], kv0.at[2 * core], fs_sem.at[9], fr_sem.at[9], {"seq": peer}).start()
+    remote(kv0.at[1], kv0.at[2 - 2 * core], fs_sem.at[10], fr_sem.at[10], {"seq": across}).start()
 
     def store_q(dst, q_rows, n):
         dst[...] = jnp.zeros(dst.shape, BF16)
@@ -212,13 +213,11 @@
             w_ref[:, lanes] = wb
             num[64 * h : 64 * h + 64, :] += nn(keyst[192 + 64 * h : 256 + 64 * h, :], wb)
 
-    def keep0(j):
-        if j == 1:
-            return jnp.float32(1.0)
-        inside = s > 0 if j == 0 else s < 63
-        return jnp.where(inside, jnp.float32(1.0), jnp.float32(0.0))
-
-    forward(kv0.at[1], kvt0.at[1], qm0, w0.at[1], num0, den0, keep0(1), 256)
+    near, far = 2 - 2 * core, 2 * core
+    outside = ((s == 0) & (core == 0)) | ((s == 63) & (core == 1))
+    far_keep = jnp.where(outside, jnp.float32(0.0), jnp.float32(1.0))
+    one = jnp.float32(1.0)
+    forward(kv0.at[1], kvt0.at[1], qm0, w0.at[1], num0, den0, one, 256)
 
     loads[3].wait()
     loads[4].wait()
@@ -227,11 +226,18 @@
     for half in range(2):
         index = iota((384, 768), 0)
         twelfth = (index * 5462) >> 16
-        feature = (twelfth & 7) * 96 + (twelfth >> 3) * 24 + half * 12 + (index - 12 * twelfth)
+        rest = half * 12 + (index - 12 * twelfth)
+        feature = (twelfth >> 2) * 96 + (twelfth & 3) * 24 + rest
         pick = one_hot(feature == iota((384, 768), 1))
         tg[half, :, 0:256] = nt(pick, tok_p).astype(BF16)
         tg[half, :, 256:512] = nt(pick, gy_p).astype(BF16)
+        feature = (twelfth & 7) * 96 + (twelfth >> 3) * 24 + rest
+        pick = one_hot(feature == iota((384, 768), 1))
+        tg[half, :, 512:768] = nt(pick, tok_p).astype(BF16)
     remote(tg.at[1 - core], ptg, cs_sem.at[0], cr_sem.at[0], {"seq": peer}).start()
+
+    arrived(kv0.at[near], fr_sem.at[9], fs_sem.at[9])
+    forward(kv0.at[near], kvt0.at[near], qm0, w0.at[near], num0, den0, one, 256)
 
     same = one_hot(iota((256, 256), 0) == iota((256, 256), 1))
     for n in range(3):
@@ -242,13 +248,13 @@
 
     half = core * 64
     other = 64 - half
-    arrived(kvc.at[0], fr_sem.at[0], fs_sem.at[0])
-    arrived(kvc.at[1], fr_sem.at[1], fs_sem.at[1])
-    remote(kvc.at[core], kvc.at[2], hs_sem.at[2], hr_sem.at[2], {"seq": peer}).start()
     for i in range(3, 9):
         piece = kvc.at[i, pl.ds(half, 64)]
         arrived(piece, fr_sem.at[i], fs_sem.at[i])
         remote(piece, piece, hs_sem.at[i], hr_sem.at[i], {"seq": peer}).start()
+    arrived(kvc.at[0], fr_sem.at[0], fs_sem.at[0])
+    arrived(kvc.at[1], fr_sem.at[1], fs_sem.at[1])
+    remote(kvc.at[core], kvc.at[2], hs_sem.at[2], hr_sem.at[2], {"seq": peer}).start()
 
     def coarse_forward(lv, j):
         i = 3 * lv + j
@@ -257,16 +263,15 @@
         factor = jnp.where(inside, jnp.float32(2 << lv), jnp.float32(0.0))
         forward(kvc.at[i], kvtc.at[i], qmc.at[lv], wc.at[i], numc, denc, factor, 128)
 
-    coarse_forward(0, 0)
-    coarse_forward(0, 1)
-    for j in (0, 2):
-        arrived(kv0.at[j], fr_sem.at[9 + j // 2], fs_sem.at[9 + j // 2])
-        forward(kv0.at[j], kvt0.at[j], qm0, w0.at[j], num0, den0, keep0(j), 256)
-    arrived(kvc.at[2], hr_sem.at[2], hs_sem.at[2])
-    coarse_forward(0, 2)
     for i in range(3, 9):
         arrived(kvc.at[i, pl.ds(other, 64)], hr_sem.at[i], hs_sem.at[i])
         coarse_forward(i // 3, i % 3)
+    coarse_forward(0, 0)
+    coarse_forward(0, 1)
+    arrived(kvc.at[2], hr_sem.at[2], hs_sem.at[2])
+    coarse_forward(0, 2)
+    arrived(kv0.at[far], fr_sem.at[10], fs_sem.at[10])
+    forward(kv0.at[far], kvt0.at[far], qm0, w0.at[far], num0, den0, far_keep, 256)
 
     lane = iota((1, 128), 1)
     gm0[...] = jnp.zeros(gm0.shape, BF16)
@@ -353,32 +358,24 @@
             {"seq": where},
         ).start()
 
-    def near_backward(j):
-        dsend0[j // 2] = backward(
-            kv0.at[j], kvt0.at[j], qm0, gm0, c0, w0.at[j], dq0, 256
+    def near_backward(slot, n, where):
+        dsend0[n] = backward(
+            kv0.at[slot], kvt0.at[slot], qm0, gm0, c0, w0.at[slot], dq0, 256
         ).astype(BF16)
-        k = 1 - j // 2
-        remote(
-            dsend0.at[j // 2], ret0.at[k], bs_sem.at[9 + k], br_sem.at[9 + k],
-            {"seq": prev_dev if j == 0 else next_dev},
-        ).start()
-
-    for i in range(6, 9):
-        to_peer(i)
-    for i in range(3, 6):
+        remote(dsend0.at[n], ret0.at[n], bs_sem.at[9 + n], br_sem.at[9 + n], {"seq": where}).start()
+
+    near_backward(far, 1, across)
+    for i in range(3, 9):
         to_peer(i)
     own1[...] = coarse_backward(0, 2).astype(BF16)
     remote(own1, sib1, ss_sem.at[2], sr_sem.at[2], {"seq": peer}).start()
+    for i in range(3, 9):
+        return_pair(i)
     return_first(1 - core, coarse_backward(0, 1 - core))
-    for i in range(6, 9):
-        return_pair(i)
     shared = coarse_backward(0, core)
-    for i in range(3, 6):
-        return_pair(i)
     arrived(sib1, sr_sem.at[2], ss_sem.at[2])
     return_first(core, shared + sib1[...].astype(F32))
-    near_backward(0)
-    near_backward(2)
+    near_backward(near, 0, peer)
     down[...] = backward(kv0.at[1], kvt0.at[1], qm0, gm0, c0, w0.at[1], dq0, 256)
 
     def spread(grad, lv):
@@ -409,43 +406,48 @@
     for j in range(4):
         gtacc[j] = nn(wqt[192 * j : 192 * j + 192, :], dq_t)
 
-    def y_stage(r, total):
+    def widen(blocks):
+        at = iota((16 * blocks, 12 * blocks), 0)
+        here = (at >> 4) * 12 + (at & 15) == iota((16 * blocks, 12 * blocks), 1)
+        return one_hot(here & ((at & 15) < 12))
+
+    first_z = ((z, 8, z_dev, zra, zs_sem, zr_sem, 0), (y, 4, y_dev, yra, ys_sem, yr_sem, 0))
+    first_y = ((y, 4, y_dev, yrb, ys_sem, yr_sem, 3), (z, 8, z_dev, zrb, zs_sem, zr_sem, 7))
+
+    def spread_out(src, rows, axis):
+        index, count, device, got, send, recv, base = axis
+        for k in range(1, count):
+            remote(
+                src.at[pl.ds(lax.rem(index + k, count) * rows, rows)], got.at[k - 1],
+                send.at[base + k - 1], recv.at[base + k - 1], {"seq": device(k)},
+            ).start()
+
+    def gathered(own, axis):
+        index, count, device, got, send, recv, base = axis
+        for k in range(count - 1):
+            arrived(got.at[k], recv.at[base + k], send.at[base + k])
+            own += got[k].astype(F32)
+        return own
+
+    def stage_one(r, total, axes):
         gf[r] = total
         gs[r] = total.astype(BF16)
-        for k in range(1, 4):
-            remote(
-                gs.at[r, pl.ds(lax.rem(y + k, 4) * 96, 96)], yr.at[r, k - 1],
-                ys_sem.at[3 * r + k - 1], yr_sem.at[3 * r + k - 1], {"seq": y_dev(k)},
-            ).start()
-
-    at16 = iota((128, 96), 0)
-    widen = one_hot(
-        ((at16 >> 4) * 12 + (at16 & 15) == iota((128, 96), 1)) & ((at16 & 15) < 12)
-    )
-
-    def z_stage(r):
-        total = gf[r, pl.ds(y * 96, 96), :]
-        for k in range(3):
-            arrived(yr.at[r, k], yr_sem.at[3 * r + k], ys_sem.at[3 * r + k])
-            total += yr[r, k].astype(F32)
-        zs[r] = nn(widen, total.astype(BF16)).astype(BF16)
-        for k in range(1, 8):
-            remote(
-                zs.at[r, pl.ds(lax.rem(z + k, 8) * 16, 16)], zr.at[r, k - 1],
-                zs_sem.at[7 * r + k - 1], zr_sem.at[7 * r + k - 1], {"seq": z_dev(k)},
-            ).start()
-
-    def z_finish(r):
-        total = zs[r, pl.ds(z * 16, 16), :].astype(F32)
-        for k in range(7):
-            arrived(zr.at[r, k], zr_sem.at[7 * r + k], zs_sem.at[7 * r + k])
-            total += zr[r, k].astype(F32)
-        return total * NORM
+        spread_out(gs.at[r], 384 // axes[0][1], axes[0])
+
+    def stage_two(r, wide_s, axes):
+        rows = 384 // axes[0][1]
+        total = gathered(gf[r, pl.ds(axes[0][0] * rows, rows), :], axes[0])
+        wide_s[...] = nn(widen(axes[1][1]), total.astype(BF16)).astype(BF16)
+        spread_out(wide_s, 16, axes[1])
+
+    def stage_end(wide_s, axes):
+        own = wide_s[pl.ds(axes[1][0] * 16, 16), :].astype(F32)
+        return gathered(own, axes[1]) * NORM
 
     arrived(ptg, cr_sem.at[0], cs_sem.at[0])
     arrived(pra.at[pl.ds(192, 192), pl.ds(256, 256)], cr_sem.at[1], cs_sem.at[1])
     arrived(pra.at[pl.ds(0, 192), pl.ds(0, 256)], cr_sem.at[2], cs_sem.at[2])
-    y_stage(0, nt(tg[core], ra[...]) + nt(ptg[...], pra[...]))
+    stage_one(0, nt(tg[core, :, 0:512], ra[...]) + nt(ptg[:, 0:512], pra[...]), first_z)
 
     def received(lv):
         if lv == 0:
@@ -484,6 +486,9 @@
     remote(dkvt, pdkvt, cs_sem.at[3], cr_sem.at[3], {"seq": peer}).start()
 
     dkv_t = dkvt[...]
+    own_part = nt(tg[core, :, 512:768], dkv_t)
+    arrived(pdkvt, cr_sem.at[3], cs_sem.at[3])
+    stage_one(1, own_part + nt(ptg[:, 512:768], pdkvt[...]), first_y)
     for j in range(4):
         gts[j] = (nn(wkvt[192 * j : 192 * j + 192, :], dkv_t) + gtacc[j]).astype(BF16)
     for k in range(1, 4):
@@ -491,10 +496,7 @@
             gts.at[mp_dev(k)], gtr.at[k - 1], ms_sem.at[2 + k], mr_sem.at[2 + k],
             {"mp": mp_dev(k)},
         ).start()
-    z_stage(0)
-    first = nt(tg[core, :, 0:256], dkvt[...])
-    arrived(pdkvt, cr_sem.at[3], cs_sem.at[3])
-    y_stage(1, first + nt(ptg[:, 0:256], pdkvt[...]))
+    stage_two(0, wsa, first_z)
 
     def mp_finish(sent, got, base, out):
         total = sent[m].astype(F32)
@@ -504,12 +506,12 @@
         out[...] = nn(total.astype(BF16), perm_s[...]).astype(BF16)
 
     mp_finish(mixs, mixr, 0, mixed_ref)
-    z_stage(1)
-    mp_finish(gts, gtr, 3, gt_ref)
-    first = z_finish(0)
+    stage_two(1, wsb, first_y)
+    first = stage_end(wsa, first_z)
     go_ref[...] = pltpu.roll(first, 192, 1)[0:12, 0:192]
     gw_ref[:, 0, :] = first[0:12, 0:192]
-    second = z_finish(1)
+    mp_finish(gts, gtr, 3, gt_ref)
+    second = stage_end(wsb, first_y)
     gw_ref[:, 1, :] = second[0:12, 0:192]
     gw_ref[:, 2, :] = pltpu.roll(second, 192, 1)[0:12, 0:192]
 
@@ -531,9 +533,12 @@
     left(dkvt, cs_sem.at[3], cr_sem.at[3])
     for i in range(6):
         left(mixs.at[0], ms_sem.at[i], mr_sem.at[i])
-        left(gs.at[0, pl.ds(0, 96)], ys_sem.at[i], yr_sem.at[i])
-    for i in range(14):
-        left(zs.at[0, pl.ds(0, 16)], zs_sem.at[i], zr_sem.at[i])
+    for i in range(3):
+        left(wsa.at[pl.ds(0, 16)], ys_sem.at[i], yr_sem.at[i])
+        left(gs.at[0, pl.ds(0, 96)], ys_sem.at[3 + i], yr_sem.at[3 + i])
+    for i in range(7):
+        left(gs.at[0, pl.ds(0, 48)], zs_sem.at[i], zr_sem.at[i])
+        left(wsa.at[pl.ds(0, 16)], zs_sem.at[7 + i], zr_sem.at[7 + i])
 
 
 def deliver(*refs):
@@ -565,10 +570,10 @@
         low(2, 256, 384), low(6, 64, 384), low(2, 256, 384), low(2, 128, 384), low(6, 64, 384),
         low(128, 384), wide(6, 128, 384), low(128, 384), low(6, 64, 384),
         low(2, 128, 384), low(6, 64, 384),
-        low(2, 384, 512), low(384, 512), low(384, 512), low(384, 512), low(384, 256), low(384, 256),
+        low(2, 384, 768), low(384, 768), low(384, 512), low(384, 512), low(384, 256), low(384, 256),
         low(4, 192, 256), low(3, 192, 256), wide(4, 192, 256), low(4, 192, 256), low(3, 192, 256),
-        wide(2, 384, 384), low(2, 384, 384), low(2, 3, 96, 384), low(2, 128, 384),
-        low(2, 7, 16, 384),
+        wide(2, 384, 384), low(2, 384, 384), low(7, 48, 384), low(3, 16, 384), low(3, 96, 384),
+        low(7, 16, 384), low(64, 384), low(128, 384),
         sems(5), sems(11), sems(11), sems(9), sems(9), sems(11), sems(11), sems(9), sems(9),
         sems(4), sems(4), sems(6), sems(6), sems(6), sems(6), sems(14), sems(14),
     ]
@@ -599,6 +604,7 @@
         in_specs=[vmem] * 4,
         out_specs=(hbm,) * 4,
         scratch_shapes=[sems(4)],
+        compiler_params=pltpu.CompilerParams(vmem_limit_bytes=1024 * 1024),
     )(*results)
     return (mixed.T[None], grad_tokens.T[None], grad_wqkv, grad_wout)
 

time: 60.4 us -> 53.3 us (0.88); the launches traced: 59.6 us -> 53.1 us
  Pallas kernels: 56.5 us -> 52.5 us
  local copies, waits for them, and re-layouts: 2.47 us -> 0 us
    pallas_call x1, Pallas kernels: 54.8 us -> 51.7 us  [shards(): pl.pallas_call(kernel, out_shape=shapes, in_specs=[hbm] * 4, out_specs=(v...]
    unnamed x8 -> x0, local copies, waits for them, and re-layouts: 2.47 us -> none
    pallas_call x1, Pallas kernels: 1.66 us -> 0.72 us  [shards(): pl.pallas_call(deliver, out_shape=shapes, in_specs=[vmem] * 4, out_specs=...]
where the time goes in v3:
time: 53.3 us; the launch traced here: 53.1 us
  Pallas kernels  52.5 us (98%)
  between operations  0.64 us (1%)
    pallas_call x1, Pallas kernels, shards(): pl.pallas_call(kernel, out_shape=shapes, in_specs=[hbm] * 4, out_specs=(v...  51.7 us

profile of v3, /device:TPU:2, one launch (start us, length us, event | category | flops | bytes accessed | tf_op | source)
XLA Modules:
  0.0 53.1 jit_solution(10422276650315106846)
XLA Ops:
  0.6 51.7 %shard_map.75 = (bf16[192,256]{1,0:T(8,128)(2,1)S(1)}, bf16[192,256]{1,0:T(8,128)(2,1)S(1)}, f32[12,3,192]{2,1,0:T(4,128)S(1)}, f32[12,192]{1,0:T(8,128)S(1)}) custom-call(bf16[256,768]{1,0:T(8,128)(2,1)} %bitcast.10, bf16[576,768]{1,0:T(8,128)(2,1)} %bitcast.9, bf16[192,768]{1,0:T(8,128)(2,1)} %wout_hbm.1, bf16[256,768]{1,0:T(8,128)(2,1)} %bitcast.11), custom_call_target="tpu_custom_call" | custom-call | flops 2000000000 | bytes 4000000 | tf_op jit(solution)/shard_map/pallas_call | solution.py:586
  52.4 0.7 %shard_map.76 = (bf16[192,256]{1,0:T(8,128)(2,1)}, bf16[192,256]{1,0:T(8,128)(2,1)}, f32[12,3,192]{2,1,0:T(4,128)}, f32[12,192]{1,0:T(8,128)}) custom-call(bf16[192,256]{1,0:T(8,128)(2,1)S(1)} %get-tuple-element.12.refs_0_, bf16[192,256]{1,0:T(8,128)(2,1)S(1)} %get-tuple-element.13.refs_1_, f32[12,3,192]{2,1,0:T(4,128)S(1)} %get-tuple-element.14.refs_2_, ...), custom_call_target="tpu_custom_call" | custom-call | tf_op jit(solution)/shard_map/pallas_call | solution.py:601

commit v4 on v3

--- a/solution.py
+++ b/solution.py
@@ -60,9 +60,9 @@
     tok_ref, wqkv_ref, wout_ref, gy_ref, wot, wqt, wkvt,
     perm_s, u0, uc, kv0, kvc, ownc, kvt0, kvtc, w0, wc, qm0, qmc, gm0, gmc, c0, cc,
     num0, numc, den0, denc, dot_s, att_s, dq0, dqc, down, dsend0, dsendc, ret0, ret1, retc,
-    own1, ownf, sib1, sibc, out1, outc,
+    own1, own1f, ownf, sib1, sibc, out1, outc,
     tg, ptg, ra, pra, dkvt, pdkvt, mixs, mixr, gtacc, gts, gtr,
-    gf, gs, zra, yra, yrb, zrb, wsa, wsb,
+    gfa, gsa, wsa, zra, yra, gfb, gsb, wsb, yrb, zrb, gfc, gsc, wsc, zrc, yrc,
     in_sem, fs_sem, fr_sem, hs_sem, hr_sem, bs_sem, br_sem, ss_sem, sr_sem,
     cs_sem, cr_sem, ms_sem, mr_sem, ys_sem, yr_sem, zs_sem, zr_sem,
 ):
@@ -152,14 +152,16 @@
     key = unit(u0[192:384, :])
     v = u0[384:576, :]
     kv0[1] = jnp.concatenate([key, v], axis=0).T.astype(BF16)
+    pl.semaphore_wait(barrier, len(partners))
+
+    remote(kv0.at[1], kv0.at[2 * core], fs_sem.at[9], fr_sem.at[9], {"seq": peer}).start()
+    remote(kv0.at[1], kv0.at[2 - 2 * core], fs_sem.at[10], fr_sem.at[10], {"seq": across}).start()
     for lv in range(3):
         mean = halves(key, lv) * 0.5
         v = halves(v, lv) * ROOT_HALF
         uc[lv, 192:384, :] = mean
         key = unit(mean)
         ownc[lv] = jnp.concatenate([key, v], axis=0).T.astype(BF16)
-
-    pl.semaphore_wait(barrier, len(partners))
 
     mine = (0, core * 64, core * 64 + lax.rem(s // 2, 2) * 32)
     for lv in (2, 1, 0):
@@ -172,9 +174,6 @@
                     kvc.at[i, pl.ds(mine[lv], rows)],
                     fs_sem.at[i], fr_sem.at[i], {"seq": target(lv, j, part)},
                 ).start()
-    remote(kv0.at[1], kv0.at[2 * core], fs_sem.at[9], fr_sem.at[9], {"seq": peer}).start()
-    remote(kv0.at[1], kv0.at[2 - 2 * core], fs_sem.at[10], fr_sem.at[10], {"seq": across}).start()
-
     def store_q(dst, q_rows, n):
         dst[...] = jnp.zeros(dst.shape, BF16)
         half = (q_rows * 0.5).astype(BF16)
@@ -201,23 +200,31 @@
     pra[0:192, 256:512] = jnp.zeros((192, 256), BF16)
     pra[192:384, 0:256] = jnp.zeros((192, 256), BF16)
 
-    def forward(keys, keyst, qm, w_ref, num, den, factor, n):
-        block = keys[...]
+    def forward(block, factors, keyst, qm, w_ref, num, den, n):
         count = block.shape[0]
-        keyst[...] = block.astype(F32).T.astype(BF16)
+        step = count // len(factors)
+        turned = block.astype(F32).T.astype(BF16)
+        keyst[...] = turned
+        w = jnp.exp(nn(block[:, 0:256], qm[...]))
+        w = jnp.concatenate(
+            [w[step * k : step * k + step] * factor for k, factor in enumerate(factors)], axis=0
+        )
+        den[...] += jnp.sum(w.reshape(count // 8, 8, 3 * n), axis=0)
+        wb = w.astype(BF16)
+        w_ref[...] = wb
         for h in range(3):
-            lanes = slice(h * n, h * n + n)
-            w = jnp.exp(nn(block[:, 0:256], qm[:, lanes])) * factor
-            den[:, lanes] += jnp.sum(w.reshape(count // 8, 8, n), axis=0)
-            wb = w.astype(BF16)
-            w_ref[:, lanes] = wb
-            num[64 * h : 64 * h + 64, :] += nn(keyst[192 + 64 * h : 256 + 64 * h, :], wb)
+            num[64 * h : 64 * h + 64, :] += nn(
+                turned[192 + 64 * h : 256 + 64 * h], wb[:, h * n : h * n + n]
+            )
+
+    def near_forward(slot, factor):
+        forward(kv0[slot], [factor], kvt0.at[slot], qm0, w0.at[slot], num0, den0, 256)
 
     near, far = 2 - 2 * core, 2 * core
     outside = ((s == 0) & (core == 0)) | ((s == 63) & (core == 1))
     far_keep = jnp.where(outside, jnp.float32(0.0), jnp.float32(1.0))
     one = jnp.float32(1.0)
-    forward(kv0.at[1], kvt0.at[1], qm0, w0.at[1], num0, den0, one, 256)
+    near_forward(1, one)
 
     loads[3].wait()
     loads[4].wait()
@@ -237,7 +244,7 @@
     remote(tg.at[1 - core], ptg, cs_sem.at[0], cr_sem.at[0], {"seq": peer}).start()
 
     arrived(kv0.at[near], fr_sem.at[9], fs_sem.at[9])
-    forward(kv0.at[near], kvt0.at[near], qm0, w0.at[near], num0, den0, one, 256)
+    near_forward(near, one)
 
     same = one_hot(iota((256, 256), 0) == iota((256, 256), 1))
     for n in range(3):
@@ -248,6 +255,8 @@
 
     half = core * 64
     other = 64 - half
+    arrived(kv0.at[far], fr_sem.at[10], fs_sem.at[10])
+    near_forward(far, far_keep)
     for i in range(3, 9):
         piece = kvc.at[i, pl.ds(half, 64)]
         arrived(piece, fr_sem.at[i], fs_sem.at[i])
@@ -256,22 +265,21 @@
     arrived(kvc.at[1], fr_sem.at[1], fs_sem.at[1])
     remote(kvc.at[core], kvc.at[2], hs_sem.at[2], hr_sem.at[2], {"seq": peer}).start()
 
-    def coarse_forward(lv, j):
-        i = 3 * lv + j
-        place = position[lv] + offset(lv, j)
-        inside = (place >= 0) & (place < extent[lv])
-        factor = jnp.where(inside, jnp.float32(2 << lv), jnp.float32(0.0))
-        forward(kvc.at[i], kvtc.at[i], qmc.at[lv], wc.at[i], numc, denc, factor, 128)
-
-    for i in range(3, 9):
-        arrived(kvc.at[i, pl.ds(other, 64)], hr_sem.at[i], hs_sem.at[i])
-        coarse_forward(i // 3, i % 3)
-    coarse_forward(0, 0)
-    coarse_forward(0, 1)
+    def coarse_forward(lv):
+        factors = []
+        for j in range(3):
+            place = position[lv] + offset(lv, j)
+            inside = (place >= 0) & (place < extent[lv])
+            factors.append(jnp.where(inside, jnp.float32(2 << lv), jnp.float32(0.0)))
+        block = kvc[3 * lv : 3 * lv + 3].reshape(384, 384)
+        forward(block, factors, kvtc.at[lv], qmc.at[lv], wc.at[lv], numc, denc, 128)
+
+    for lv in (2, 1):
+        for i in range(3 * lv, 3 * lv + 3):
+            arrived(kvc.at[i, pl.ds(other, 64)], hr_sem.at[i], hs_sem.at[i])
+        coarse_forward(lv)
     arrived(kvc.at[2], hr_sem.at[2], hs_sem.at[2])
-    coarse_forward(0, 2)
-    arrived(kv0.at[far], fr_sem.at[10], fs_sem.at[10])
-    forward(kv0.at[far], kvt0.at[far], qm0, w0.at[far], num0, den0, far_keep, 256)
+    coarse_forward(0)
 
     lane = iota((1, 128), 1)
     gm0[...] = jnp.zeros(gm0.shape, BF16)
@@ -307,48 +315,45 @@
         cs_sem.at[1], cr_sem.at[1], {"seq": peer},
     ).start()
 
-    def backward(keys, keyst, qm, gm, c_rows, w_ref, dq, n):
-        count = keys.shape[0]
-        dk = jnp.zeros((count, 256), F32)
-        dv = jnp.zeros((count, 256), F32)
+    def backward(block, keyst, qm, gm, c_rows, w_ref, dq, n):
+        wb = w_ref[...]
+        inner = nn(block[:, 128:384], gm[...])
+        slope = (wb.astype(F32) * (inner - c_rows[0:1, :])).astype(BF16)
+        dk = nt(slope, qm[...])
+        dv = nt(wb, gm[...])
         for h in range(3):
-            lanes = slice(h * n, h * n + n)
-            wb = w_ref[:, lanes]
-            inner = nn(keys[:, 128:384], gm[:, lanes])
-            slope = (wb.astype(F32) * (inner - c_rows[0:1, lanes])).astype(BF16)
-            dq[64 * h : 64 * h + 64, :] += nn(keyst[64 * h : 64 * h + 64, :], slope)
-            dk += nt(slope, qm[:, lanes])
-            dv += nt(wb, gm[:, lanes])
+            dq[64 * h : 64 * h + 64, :] += nn(
+                keyst[64 * h : 64 * h + 64, :], slope[:, h * n : h * n + n]
+            )
         return jnp.concatenate(
             [dk[:, 0:128], dk[:, 128:256] + dv[:, 0:128], dv[:, 128:256]], axis=1
         )
 
-    def coarse_backward(lv, i):
+    def coarse_backward(lv):
+        block = kvc[3 * lv : 3 * lv + 3].reshape(384, 384)
         return backward(
-            kvc.at[i], kvtc.at[i], qmc.at[lv], gmc.at[lv], cc.at[lv], wc.at[i], dqc.at[lv], 128
+            block, kvtc.at[lv], qmc.at[lv], gmc.at[lv], cc.at[lv], wc.at[lv], dqc.at[lv], 128
         )
 
-    def to_peer(i):
-        ownf[i - 3] = coarse_backward(i // 3, i)
-        dsendc[i - 3] = ownf[i - 3, pl.ds(other, 64), :].astype(BF16)
+    def to_peer(lv):
+        ownf[lv - 1] = coarse_backward(lv).reshape(3, 2, 64, 384)
+        dsendc[lv - 1] = ownf[lv - 1, :, 1 - core].astype(BF16)
         remote(
-            dsendc.at[i - 3], sibc.at[i - 3], ss_sem.at[i], sr_sem.at[i], {"seq": peer}
+            dsendc.at[lv - 1], sibc.at[lv - 1], ss_sem.at[lv], sr_sem.at[lv], {"seq": peer}
         ).start()
 
-    def return_pair(i):
-        lv, j = i // 3, i % 3
-        arrived(sibc.at[i - 3], sr_sem.at[i], ss_sem.at[i])
-        outc[i - 3] = (
-            ownf[i - 3, pl.ds(half, 64), :] + sibc[i - 3].astype(F32)
-        ).astype(BF16)
-        k = 3 * lv + back_slot(j)
+    def return_pairs(lv):
+        arrived(sibc.at[lv - 1], sr_sem.at[lv], ss_sem.at[lv])
+        outc[lv - 1] = (ownf[lv - 1, :, core] + sibc[lv - 1].astype(F32)).astype(BF16)
         rows = 128 >> lv
         into = 0 if lv == 1 else lax.rem(s // 2, 2) * 32
-        for part in range(parts(lv)):
-            remote(
-                outc.at[i - 3, pl.ds(part * rows, rows)], retc.at[k - 3, pl.ds(into, rows)],
-                bs_sem.at[k], br_sem.at[k], {"seq": target(lv, j, part)},
-            ).start()
+        for j in range(3):
+            k = 3 * lv + back_slot(j)
+            for part in range(parts(lv)):
+                remote(
+                    outc.at[lv - 1, j, pl.ds(part * rows, rows)], retc.at[k - 3, pl.ds(into, rows)],
+                    bs_sem.at[k], br_sem.at[k], {"seq": target(lv, j, part)},
+                ).start()
 
     def return_first(slot, value):
         out1[slot] = value.astype(BF16)
@@ -358,25 +363,26 @@
             {"seq": where},
         ).start()
 
-    def near_backward(slot, n, where):
-        dsend0[n] = backward(
-            kv0.at[slot], kvt0.at[slot], qm0, gm0, c0, w0.at[slot], dq0, 256
-        ).astype(BF16)
+    def near_backward(slot):
+        return backward(kv0[slot], kvt0.at[slot], qm0, gm0, c0, w0.at[slot], dq0, 256)
+
+    def return_near(slot, n, where):
+        dsend0[n] = near_backward(slot).astype(BF16)
         remote(dsend0.at[n], ret0.at[n], bs_sem.at[9 + n], br_sem.at[9 + n], {"seq": where}).start()
 
-    near_backward(far, 1, across)
-    for i in range(3, 9):
-        to_peer(i)
-    own1[...] = coarse_backward(0, 2).astype(BF16)
-    remote(own1, sib1, ss_sem.at[2], sr_sem.at[2], {"seq": peer}).start()
-    for i in range(3, 9):
-        return_pair(i)
-    return_first(1 - core, coarse_backward(0, 1 - core))
-    shared = coarse_backward(0, core)
-    arrived(sib1, sr_sem.at[2], ss_sem.at[2])
-    return_first(core, shared + sib1[...].astype(F32))
-    near_backward(near, 0, peer)
-    down[...] = backward(kv0.at[1], kvt0.at[1], qm0, gm0, c0, w0.at[1], dq0, 256)
+    return_near(far, 1, across)
+    to_peer(2)
+    to_peer(1)
+    own1f[...] = coarse_backward(0).reshape(3, 128, 384)
+    own1[...] = own1f[2].astype(BF16)
+    remote(own1, sib1, ss_sem.at[0], sr_sem.at[0], {"seq": peer}).start()
+    return_pairs(2)
+    return_pairs(1)
+    return_first(1 - core, own1f[1 - core])
+    arrived(sib1, sr_sem.at[0], ss_sem.at[0])
+    return_first(core, own1f[core] + sib1[...].astype(F32))
+    return_near(near, 0, peer)
+    down[...] = near_backward(1)
 
     def spread(grad, lv):
         if lv == 0:
@@ -411,8 +417,18 @@
         here = (at >> 4) * 12 + (at & 15) == iota((16 * blocks, 12 * blocks), 1)
         return one_hot(here & ((at & 15) < 12))
 
-    first_z = ((z, 8, z_dev, zra, zs_sem, zr_sem, 0), (y, 4, y_dev, yra, ys_sem, yr_sem, 0))
-    first_y = ((y, 4, y_dev, yrb, ys_sem, yr_sem, 3), (z, 8, z_dev, zrb, zs_sem, zr_sem, 7))
+    part_a = (
+        gfa, gsa, wsa,
+        ((z, 8, z_dev, zra, zs_sem, zr_sem, 0), (y, 4, y_dev, yra, ys_sem, yr_sem, 0)),
+    )
+    part_b = (
+        gfb, gsb, wsb,
+        ((y, 4, y_dev, yrb, ys_sem, yr_sem, 3), (z, 8, z_dev, zrb, zs_sem, zr_sem, 7)),
+    )
+    part_c = (
+        gfc, gsc, wsc,
+        ((z, 8, z_dev, zrc, zs_sem, zr_sem, 14), (y, 4, y_dev, yrc, ys_sem, yr_sem, 6)),
+    )
 
     def spread_out(src, rows, axis):
         index, count, device, got, send, recv, base = axis
@@ -429,25 +445,35 @@
             own += got[k].astype(F32)
         return own
 
-    def stage_one(r, total, axes):
-        gf[r] = total
-        gs[r] = total.astype(BF16)
-        spread_out(gs.at[r], 384 // axes[0][1], axes[0])
-
-    def stage_two(r, wide_s, axes):
+    def stage_one(part, total):
+        whole, low_s, wide_s, axes = part
+        whole[...] = total
+        low_s[...] = total.astype(BF16)
+        spread_out(low_s, 384 // axes[0][1], axes[0])
+
+    def stage_two(part):
+        whole, low_s, wide_s, axes = part
         rows = 384 // axes[0][1]
-        total = gathered(gf[r, pl.ds(axes[0][0] * rows, rows), :], axes[0])
+        total = gathered(whole[pl.ds(axes[0][0] * rows, rows), :], axes[0])
         wide_s[...] = nn(widen(axes[1][1]), total.astype(BF16)).astype(BF16)
         spread_out(wide_s, 16, axes[1])
 
-    def stage_end(wide_s, axes):
+    def stage_end(part):
+        whole, low_s, wide_s, axes = part
         own = wide_s[pl.ds(axes[1][0] * 16, 16), :].astype(F32)
         return gathered(own, axes[1]) * NORM
+
+    def stage_left(part):
+        whole, low_s, wide_s, axes = part
+        for rows, src, axis in ((384 // axes[0][1], low_s, axes[0]), (16, wide_s, axes[1])):
+            index, count, device, got, send, recv, base = axis
+            for k in range(count - 1):
+                left(src.at[pl.ds(0, rows)], send.at[base + k], recv.at[base + k])
 
     arrived(ptg, cr_sem.at[0], cs_sem.at[0])
     arrived(pra.at[pl.ds(192, 192), pl.ds(256, 256)], cr_sem.at[1], cs_sem.at[1])
     arrived(pra.at[pl.ds(0, 192), pl.ds(0, 256)], cr_sem.at[2], cs_sem.at[2])
-    stage_one(0, nt(tg[core, :, 0:512], ra[...]) + nt(ptg[:, 0:512], pra[...]), first_z)
+    stage_one(part_a, nt(tg[core, :, 0:512], ra[...]) + nt(ptg[:, 0:512], pra[...]))
 
     def received(lv):
         if lv == 0:
@@ -486,9 +512,11 @@
     remote(dkvt, pdkvt, cs_sem.at[3], cr_sem.at[3], {"seq": peer}).start()
 
     dkv_t = dkvt[...]
-    own_part = nt(tg[core, :, 512:768], dkv_t)
+    own_b = nt(tg[core, :, 512:768], dkv_t[0:256])
+    own_c = nt(tg[core, :, 0:256], dkv_t[256:384])
     arrived(pdkvt, cr_sem.at[3], cs_sem.at[3])
-    stage_one(1, own_part + nt(ptg[:, 512:768], pdkvt[...]), first_y)
+    stage_one(part_b, own_b + nt(ptg[:, 512:768], pdkvt[0:256, :]))
+    stage_one(part_c, own_c + nt(ptg[:, 0:256], pdkvt[256:384, :]))
     for j in range(4):
         gts[j] = (nn(wkvt[192 * j : 192 * j + 192, :], dkv_t) + gtacc[j]).astype(BF16)
     for k in range(1, 4):
@@ -496,7 +524,7 @@
             gts.at[mp_dev(k)], gtr.at[k - 1], ms_sem.at[2 + k], mr_sem.at[2 + k],
             {"mp": mp_dev(k)},
         ).start()
-    stage_two(0, wsa, first_z)
+    stage_two(part_a)
 
     def mp_finish(sent, got, base, out):
         total = sent[m].astype(F32)
@@ -506,12 +534,14 @@
         out[...] = nn(total.astype(BF16), perm_s[...]).astype(BF16)
 
     mp_finish(mixs, mixr, 0, mixed_ref)
-    stage_two(1, wsb, first_y)
-    first = stage_end(wsa, first_z)
+    stage_two(part_b)
+    stage_two(part_c)
+    first = stage_end(part_a)
     go_ref[...] = pltpu.roll(first, 192, 1)[0:12, 0:192]
     gw_ref[:, 0, :] = first[0:12, 0:192]
     mp_finish(gts, gtr, 3, gt_ref)
-    second = stage_end(wsb, first_y)
+    third = stage_end(part_c)
+    second = jnp.concatenate([stage_end(part_b), third], axis=1)
     gw_ref[:, 1, :] = second[0:12, 0:192]
     gw_ref[:, 2, :] = pltpu.roll(second, 192, 1)[0:12, 0:192]
 
@@ -521,24 +551,21 @@
         left(dsend0.at[i], fs_sem.at[9 + i], fr_sem.at[9 + i])
         left(dsend0.at[i], bs_sem.at[9 + i], br_sem.at[9 + i])
     left(own1, hs_sem.at[2], hr_sem.at[2])
-    left(own1, ss_sem.at[2], sr_sem.at[2])
+    left(own1, ss_sem.at[0], sr_sem.at[0])
+    for lv in (1, 2):
+        left(dsendc.at[0], ss_sem.at[lv], sr_sem.at[lv])
     for i in range(3, 9):
-        left(outc.at[i - 3], fs_sem.at[i], fr_sem.at[i])
-        left(outc.at[i - 3], hs_sem.at[i], hr_sem.at[i])
-        left(outc.at[i - 3], ss_sem.at[i], sr_sem.at[i])
-        left(outc.at[i - 3], bs_sem.at[i], br_sem.at[i])
+        left(outc.at[0, 0], fs_sem.at[i], fr_sem.at[i])
+        left(outc.at[0, 0], hs_sem.at[i], hr_sem.at[i])
+        left(outc.at[0, 0], bs_sem.at[i], br_sem.at[i])
     left(ptg, cs_sem.at[0], cr_sem.at[0])
     left(ra.at[pl.ds(192, 192), pl.ds(256, 256)], cs_sem.at[1], cr_sem.at[1])
     left(ra.at[pl.ds(0, 192), pl.ds(0, 256)], cs_sem.at[2], cr_sem.at[2])
     left(dkvt, cs_sem.at[3], cr_sem.at[3])
     for i in range(6):
         left(mixs.at[0], ms_sem.at[i], mr_sem.at[i])
-    for i in range(3):
-        left(wsa.at[pl.ds(0, 16)], ys_sem.at[i], yr_sem.at[i])
-        left(gs.at[0, pl.ds(0, 96)], ys_sem.at[3 + i], yr_sem.at[3 + i])
-    for i in range(7):
-        left(gs.at[0, pl.ds(0, 48)], zs_sem.at[i], zr_sem.at[i])
-        left(wsa.at[pl.ds(0, 16)], zs_sem.at[7 + i], zr_sem.at[7 + i])
+    for part in (part_a, part_b, part_c):
+        stage_left(part)
 
 
 def deliver(*refs):
@@ -562,20 +589,21 @@
         low(256, 768), low(576, 768), low(192, 768), low(256, 768),
         low(768, 192), low(768, 192), low(768, 384),
         low(256, 256), wide(576, 256), wide(3, 384, 128),
-        low(3, 256, 384), low(9, 128, 384), low(3, 128, 384), low(3, 384, 256), low(9, 384, 128),
-        low(3, 256, 768), low(9, 128, 384), low(256, 768), low(3, 256, 384),
+        low(3, 256, 384), low(9, 128, 384), low(3, 128, 384), low(3, 384, 256), low(3, 384, 384),
+        low(3, 256, 768), low(3, 384, 384), low(256, 768), low(3, 256, 384),
         low(256, 768), low(3, 256, 384), wide(8, 768), wide(3, 8, 384),
         wide(192, 256), wide(192, 128), wide(8, 768), wide(8, 384), low(192, 256), low(192, 256),
         wide(192, 256), wide(3, 192, 128), wide(256, 384),
-        low(2, 256, 384), low(6, 64, 384), low(2, 256, 384), low(2, 128, 384), low(6, 64, 384),
-        low(128, 384), wide(6, 128, 384), low(128, 384), low(6, 64, 384),
-        low(2, 128, 384), low(6, 64, 384),
+        low(2, 256, 384), low(2, 3, 64, 384), low(2, 256, 384), low(2, 128, 384), low(6, 64, 384),
+        low(128, 384), wide(3, 128, 384), wide(2, 3, 2, 64, 384), low(128, 384), low(2, 3, 64, 384),
+        low(2, 128, 384), low(2, 3, 64, 384),
         low(2, 384, 768), low(384, 768), low(384, 512), low(384, 512), low(384, 256), low(384, 256),
         low(4, 192, 256), low(3, 192, 256), wide(4, 192, 256), low(4, 192, 256), low(3, 192, 256),
-        wide(2, 384, 384), low(2, 384, 384), low(7, 48, 384), low(3, 16, 384), low(3, 96, 384),
-        low(7, 16, 384), low(64, 384), low(128, 384),
-        sems(5), sems(11), sems(11), sems(9), sems(9), sems(11), sems(11), sems(9), sems(9),
-        sems(4), sems(4), sems(6), sems(6), sems(6), sems(6), sems(14), sems(14),
+        wide(384, 384), low(384, 384), low(64, 384), low(7, 48, 384), low(3, 16, 384),
+        wide(384, 256), low(384, 256), low(128, 256), low(3, 96, 256), low(7, 16, 256),
+        wide(384, 128), low(384, 128), low(64, 128), low(7, 48, 128), low(3, 16, 128),
+        sems(5), sems(11), sems(11), sems(9), sems(9), sems(11), sems(11), sems(3), sems(3),
+        sems(4), sems(4), sems(6), sems(6), sems(9), sems(9), sems(21), sems(21),
     ]
     shapes = (
         jax.ShapeDtypeStruct((192, 256), BF16),

time: 53.3 us -> 49.6 us (0.931); the launches traced: 53.1 us -> 48.7 us
  Pallas kernels: 52.5 us -> 48.1 us
    pallas_call x1, Pallas kernels: 51.7 us -> 47.4 us  [shards(): pl.pallas_call(kernel, out_shape=shapes, in_specs=[hbm] * 4, out_specs=(v...]
where the time goes in v4:
time: 49.6 us; the launch traced here: 48.7 us
  Pallas kernels  48.1 us (97%)
  between operations  0.64 us (1%)
    pallas_call x1, Pallas kernels, shards(): pl.pallas_call(kernel, out_shape=shapes, in_specs=[hbm] * 4, out_specs=(v...  47.4 us

profile of v4, /device:TPU:2, one launch (start us, length us, event | category | flops | bytes accessed | tf_op | source)
XLA Modules:
  0.0 48.7 jit_solution(16469776767625064879)
XLA Ops:
  0.6 47.4 %shard_map.75 = (bf16[192,256]{1,0:T(8,128)(2,1)S(1)}, bf16[192,256]{1,0:T(8,128)(2,1)S(1)}, f32[12,3,192]{2,1,0:T(4,128)S(1)}, f32[12,192]{1,0:T(8,128)S(1)}) custom-call(bf16[256,768]{1,0:T(8,128)(2,1)} %bitcast.10, bf16[576,768]{1,0:T(8,128)(2,1)} %bitcast.9, bf16[192,768]{1,0:T(8,128)(2,1)} %wout_hbm.1, bf16[256,768]{1,0:T(8,128)(2,1)} %bitcast.11), custom_call_target="tpu_custom_call" | custom-call | flops 2000000000 | bytes 4000000 | tf_op jit(solution)/shard_map/pallas_call | solution.py:614
  48.0 0.7 %shard_map.76 = (bf16[192,256]{1,0:T(8,128)(2,1)}, bf16[192,256]{1,0:T(8,128)(2,1)}, f32[12,3,192]{2,1,0:T(4,128)}, f32[12,192]{1,0:T(8,128)}) custom-call(bf16[192,256]{1,0:T(8,128)(2,1)S(1)} %get-tuple-element.12.refs_0_, bf16[192,256]{1,0:T(8,128)(2,1)S(1)} %get-tuple-element.13.refs_1_, f32[12,3,192]{2,1,0:T(4,128)S(1)} %get-tuple-element.14.refs_2_, ...), custom_call_target="tpu_custom_call" | custom-call | tf_op jit(solution)/shard_map/pallas_call | solution.py:629

commit v5 on v4

--- a/solution.py
+++ b/solution.py
@@ -59,12 +59,13 @@
     mixed_ref, gt_ref, gw_ref, go_ref,
     tok_ref, wqkv_ref, wout_ref, gy_ref, wot, wqt, wkvt,
     perm_s, u0, uc, kv0, kvc, ownc, kvt0, kvtc, w0, wc, qm0, qmc, gm0, gmc, c0, cc,
-    num0, numc, den0, denc, dot_s, att_s, dq0, dqc, down, dsend0, dsendc, ret0, ret1, retc,
-    own1, own1f, ownf, sib1, sibc, out1, outc,
+    num0, numc, den0, denc, dot_s, att_s, dq0, dqc, down, dsend0, dsendc, ret0, retc,
+    ownf, sibc, outc,
+    q0s, q1s, q0r, q1r, g0s, g1s, g0r, g1r, qmr0, gmr0, qmr1, gmr1,
     tg, ptg, ra, pra, dkvt, pdkvt, mixs, mixr, gtacc, gts, gtr,
     gfa, gsa, wsa, zra, yra, gfb, gsb, wsb, yrb, zrb, gfc, gsc, wsc, zrc, yrc,
     in_sem, fs_sem, fr_sem, hs_sem, hr_sem, bs_sem, br_sem, ss_sem, sr_sem,
-    cs_sem, cr_sem, ms_sem, mr_sem, ys_sem, yr_sem, zs_sem, zr_sem,
+    qs_sem, qr_sem, cs_sem, cr_sem, ms_sem, mr_sem, ys_sem, yr_sem, zs_sem, zr_sem,
 ):
     loads = [
         pltpu.make_async_copy(src, dst, in_sem.at[n])
@@ -116,14 +117,14 @@
         return lax.rem(m + k, 4)
 
     barrier = pltpu.get_barrier_semaphore()
-    partners = [{"seq": prev_dev}, {"seq": next_dev}]
-    for lv in range(3):
-        for j in range(2 if lv == 0 else 3):
+    partners = [{"seq": z_dev(k)} for k in (4, 3, 5, 2, 6, 1, 7)]
+    for lv in (2, 1, 0):
+        for j in range(3):
             for part in range(parts(lv)):
                 partners.append({"seq": target(lv, j, part)})
-    partners += [{"seq": y_dev(k)} for k in range(1, 4)]
-    partners += [{"seq": z_dev(k)} for k in range(1, 8)]
-    partners += [{"mp": mp_dev(k)} for k in range(1, 4)]
+    partners += [{"seq": y_dev(k)} for k in (2, 1, 3)]
+    partners += [{"mp": mp_dev(k)} for k in (2, 1, 3)]
+    partners += [{"seq": prev_dev}, {"seq": next_dev}]
     for partner in partners:
         pl.semaphore_signal(barrier, inc=1, device_id=partner, device_id_type=MESH)
 
@@ -184,11 +185,14 @@
     u0[0:192, :] = nt(wqkv_ref[0:192, :], tok_p)
     query = unit(u0[0:192, :])
     store_q(qm0, query, 256)
+    q0s[...] = (query * 0.5).astype(BF16)
     for lv in range(3):
         mean = halves(query, lv) * 0.5
         uc[lv, 0:192, :] = mean
         query = unit(mean)
         store_q(qmc.at[lv], query, 128)
+        if lv == 0:
+            q1s[...] = (query * 0.5).astype(BF16)
 
     num0[...] = jnp.zeros(num0.shape, F32)
     numc[...] = jnp.zeros(numc.shape, F32)
@@ -197,6 +201,8 @@
     dq0[...] = jnp.zeros(dq0.shape, F32)
     dqc[...] = jnp.zeros(dqc.shape, F32)
     ra[...] = jnp.zeros(ra.shape, BF16)
+    for ref in (qmr0, gmr0, qmr1, gmr1):
+        ref[...] = jnp.zeros(ref.shape, BF16)
     pra[0:192, 256:512] = jnp.zeros((192, 256), BF16)
     pra[192:384, 0:256] = jnp.zeros((192, 256), BF16)
 
@@ -265,12 +271,23 @@
     arrived(kvc.at[1], fr_sem.at[1], fs_sem.at[1])
     remote(kvc.at[core], kvc.at[2], hs_sem.at[2], hr_sem.at[2], {"seq": peer}).start()
 
+    def to_owners(own0, own1, got0, got1, base):
+        remote(own0, got0, qs_sem.at[base], qr_sem.at[base], {"seq": across}).start()
+        for j in range(3):
+            k = base + 1 + back_slot(j)
+            remote(
+                own1, got1.at[back_slot(j)], qs_sem.at[k], qr_sem.at[k], {"seq": target(0, j, 0)}
+            ).start()
+
+    to_owners(q0s, q1s, q0r, q1r, 0)
+
+    def level_factor(lv, j):
+        place = position[lv] + offset(lv, j)
+        inside = (place >= 0) & (place < extent[lv])
+        return jnp.where(inside, jnp.float32(2 << lv), jnp.float32(0.0))
+
     def coarse_forward(lv):
-        factors = []
-        for j in range(3):
-            place = position[lv] + offset(lv, j)
-            inside = (place >= 0) & (place < extent[lv])
-            factors.append(jnp.where(inside, jnp.float32(2 << lv), jnp.float32(0.0)))
+        factors = [level_factor(lv, j) for j in range(3)]
         block = kvc[3 * lv : 3 * lv + 3].reshape(384, 384)
         forward(block, factors, kvtc.at[lv], qmc.at[lv], wc.at[lv], numc, denc, 128)
 
@@ -284,6 +301,7 @@
     lane = iota((1, 128), 1)
     gm0[...] = jnp.zeros(gm0.shape, BF16)
     gmc[...] = jnp.zeros(gmc.shape, BF16)
+    offsets0, offsets1 = [], []
     for h in range(3):
         rows = slice(64 * h, 64 * h + 64)
         grows = slice(64 * h + 64, 64 * h + 128)
@@ -298,9 +316,13 @@
         g = d_att * inverse
         c = jnp.sum(d_att * att.astype(F32), axis=0, keepdims=True) * inverse
         gm0[grows, 256 * h : 256 * h + 256] = g.astype(BF16)
+        g0s[rows, :] = g.astype(BF16)
+        offsets0.append(c)
         c0[:, 256 * h : 256 * h + 256] = jnp.broadcast_to(c, (8, 256))
         g = g[:, 0:128] + g[:, 128:256]
         c = c[:, 0:128] + c[:, 128:256]
+        g1s[rows, :] = g.astype(BF16)
+        offsets1.append(c)
         for lv in range(3):
             if lv > 0:
                 g = g + pltpu.roll(g, 128 >> lv, 1)
@@ -310,30 +332,57 @@
             cc[lv, :, 128 * h : 128 * h + 128] = jnp.broadcast_to(
                 jnp.where(used, c, 0.0), (8, 128)
             )
+    for store, offsets in ((g0s, offsets0), (g1s, offsets1)):
+        high = [c.astype(BF16).astype(F32) for c in offsets]
+        low = [c - h for c, h in zip(offsets, high)]
+        rest = jnp.zeros((10, store.shape[1]), F32)
+        store[192:208, :] = jnp.concatenate(high + low + [rest], axis=0).astype(BF16)
+    to_owners(g0s, g1s, g0r, g1r, 4)
     remote(
         ra.at[pl.ds(192, 192), pl.ds(256, 256)], pra.at[pl.ds(192, 192), pl.ds(256, 256)],
         cs_sem.at[1], cr_sem.at[1], {"seq": peer},
     ).start()
 
-    def backward(block, keyst, qm, gm, c_rows, w_ref, dq, n):
+    def key_part(slope, wb, qm, gm):
+        dk = nt(slope, qm[...])
+        dv = nt(wb, gm[...])
+        return jnp.concatenate(
+            [dk[:, 0:128], dk[:, 128:256] + dv[:, 0:128], dv[:, 128:256]], axis=1
+        )
+
+    def backward(block, keyst, qm, gm, c_rows, w_ref, dq, n, keys=True):
         wb = w_ref[...]
         inner = nn(block[:, 128:384], gm[...])
         slope = (wb.astype(F32) * (inner - c_rows[0:1, :])).astype(BF16)
-        dk = nt(slope, qm[...])
-        dv = nt(wb, gm[...])
         for h in range(3):
             dq[64 * h : 64 * h + 64, :] += nn(
                 keyst[64 * h : 64 * h + 64, :], slope[:, h * n : h * n + n]
             )
-        return jnp.concatenate(
-            [dk[:, 0:128], dk[:, 128:256] + dv[:, 0:128], dv[:, 128:256]], axis=1
-        )
-
-    def coarse_backward(lv):
+        return key_part(slope, wb, qm, gm) if keys else None
+
+    def coarse_backward(lv, keys=True):
         block = kvc[3 * lv : 3 * lv + 3].reshape(384, 384)
         return backward(
-            block, kvtc.at[lv], qmc.at[lv], gmc.at[lv], cc.at[lv], wc.at[lv], dqc.at[lv], 128
+            block, kvtc.at[lv], qmc.at[lv], gmc.at[lv], cc.at[lv], wc.at[lv], dqc.at[lv], 128, keys
         )
+
+    def owner_backward(block, blocks, qm, gm, n):
+        c_rows = []
+        for b, (q_got, g_got, factor) in enumerate(blocks):
+            for h in range(3):
+                lanes = slice((3 * b + h) * n, (3 * b + h + 1) * n)
+                qm[64 * h : 64 * h + 64, lanes] = q_got[64 * h : 64 * h + 64, :]
+                gm[64 * h + 64 : 64 * h + 128, lanes] = g_got[64 * h : 64 * h + 64, :]
+            c = g_got[192:208, :].astype(F32)
+            c_rows += [c[h : h + 1] + c[h + 3 : h + 4] for h in range(3)]
+        w = jnp.exp(nn(block[:, 0:256], qm[...]))
+        w = jnp.concatenate(
+            [w[:, 3 * n * b : 3 * n * b + 3 * n] * blk[2] for b, blk in enumerate(blocks)], axis=1
+        )
+        wb = w.astype(BF16)
+        inner = nn(block[:, 128:384], gm[...])
+        slope = (wb.astype(F32) * (inner - jnp.concatenate(c_rows, axis=1))).astype(BF16)
+        return key_part(slope, wb, qm, gm)
 
     def to_peer(lv):
         ownf[lv - 1] = coarse_backward(lv).reshape(3, 2, 64, 384)
@@ -355,34 +404,18 @@
                     bs_sem.at[k], br_sem.at[k], {"seq": target(lv, j, part)},
                 ).start()
 
-    def return_first(slot, value):
-        out1[slot] = value.astype(BF16)
-        where = lax.rem(s + 4 * slot - 2 + 64, 64)
-        remote(
-            out1.at[slot], ret1.at[1 - slot], bs_sem.at[1 - slot], br_sem.at[1 - slot],
-            {"seq": where},
-        ).start()
-
-    def near_backward(slot):
-        return backward(kv0[slot], kvt0.at[slot], qm0, gm0, c0, w0.at[slot], dq0, 256)
-
-    def return_near(slot, n, where):
-        dsend0[n] = near_backward(slot).astype(BF16)
-        remote(dsend0.at[n], ret0.at[n], bs_sem.at[9 + n], br_sem.at[9 + n], {"seq": where}).start()
-
-    return_near(far, 1, across)
+    def near_backward(slot, keys=True):
+        return backward(kv0[slot], kvt0.at[slot], qm0, gm0, c0, w0.at[slot], dq0, 256, keys)
+
     to_peer(2)
     to_peer(1)
-    own1f[...] = coarse_backward(0).reshape(3, 128, 384)
-    own1[...] = own1f[2].astype(BF16)
-    remote(own1, sib1, ss_sem.at[0], sr_sem.at[0], {"seq": peer}).start()
+    dsend0[...] = near_backward(near).astype(BF16)
     return_pairs(2)
     return_pairs(1)
-    return_first(1 - core, own1f[1 - core])
-    arrived(sib1, sr_sem.at[0], ss_sem.at[0])
-    return_first(core, own1f[core] + sib1[...].astype(F32))
-    return_near(near, 0, peer)
+    remote(dsend0, ret0, bs_sem.at[9], br_sem.at[9], {"seq": peer}).start()
     down[...] = near_backward(1)
+    near_backward(far, False)
+    coarse_backward(0, False)
 
     def spread(grad, lv):
         if lv == 0:
@@ -477,10 +510,11 @@
 
     def received(lv):
         if lv == 0:
-            total = jnp.zeros((128, 384), F32)
-            for i in range(2):
-                arrived(ret1.at[i], br_sem.at[i], bs_sem.at[i])
-                total += ret1[i].astype(F32)
+            for j in range(3):
+                arrived(q1r.at[j], qr_sem.at[1 + j], qs_sem.at[1 + j])
+                arrived(g1r.at[j], qr_sem.at[5 + j], qs_sem.at[5 + j])
+            blocks = [(q1r.at[j], g1r.at[j], level_factor(0, j)) for j in range(3)]
+            total = owner_backward(ownc[0], blocks, qmr1, gmr1, 128)
         else:
             total = jnp.zeros((64, 384), F32)
             for i in range(3 * lv, 3 * lv + 3):
@@ -494,6 +528,9 @@
             total = jnp.concatenate([total, jnp.zeros((128 - rows, 384), F32)], axis=0)
         return total.T
 
+    arrived(q0r, qr_sem.at[0], qs_sem.at[0])
+    arrived(g0r, qr_sem.at[4], qs_sem.at[4])
+    down[...] += owner_backward(kv0[1], [(q0r, g0r, far_keep)], qmr0, gmr0, 256)
     total = received(2)
     for lv in (2, 1, 0):
         grad_k = unit_back(uc[lv, 192:384, :], total[0:192]) * 0.5
@@ -501,10 +538,8 @@
         if lv > 0:
             base = received(lv - 1)
         else:
-            base = down[...]
-            for j in range(2):
-                arrived(ret0.at[j], br_sem.at[9 + j], bs_sem.at[9 + j])
-                base += ret0[j].astype(F32)
+            arrived(ret0, br_sem.at[9], bs_sem.at[9])
+            base = down[...] + ret0[...].astype(F32)
             base = round_low(base).T
         total = base + jnp.concatenate([spread(grad_k, lv), spread(grad_v, lv)], axis=0)
     dkv = jnp.concatenate([unit_back(u0[192:384, :], total[0:192]), total[192:384]], axis=0)
@@ -524,7 +559,6 @@
             gts.at[mp_dev(k)], gtr.at[k - 1], ms_sem.at[2 + k], mr_sem.at[2 + k],
             {"mp": mp_dev(k)},
         ).start()
-    stage_two(part_a)
 
     def mp_finish(sent, got, base, out):
         total = sent[m].astype(F32)
@@ -536,22 +570,21 @@
     mp_finish(mixs, mixr, 0, mixed_ref)
     stage_two(part_b)
     stage_two(part_c)
+    stage_two(part_a)
     first = stage_end(part_a)
     go_ref[...] = pltpu.roll(first, 192, 1)[0:12, 0:192]
     gw_ref[:, 0, :] = first[0:12, 0:192]
     mp_finish(gts, gtr, 3, gt_ref)
-    third = stage_end(part_c)
-    second = jnp.concatenate([stage_end(part_b), third], axis=1)
-    gw_ref[:, 1, :] = second[0:12, 0:192]
-    gw_ref[:, 2, :] = pltpu.roll(second, 192, 1)[0:12, 0:192]
 
     for i in range(2):
-        left(out1.at[i], fs_sem.at[i], fr_sem.at[i])
-        left(out1.at[i], bs_sem.at[i], br_sem.at[i])
-        left(dsend0.at[i], fs_sem.at[9 + i], fr_sem.at[9 + i])
-        left(dsend0.at[i], bs_sem.at[9 + i], br_sem.at[9 + i])
-    left(own1, hs_sem.at[2], hr_sem.at[2])
-    left(own1, ss_sem.at[0], sr_sem.at[0])
+        left(ownc.at[0], fs_sem.at[i], fr_sem.at[i])
+        left(kv0.at[1], fs_sem.at[9 + i], fr_sem.at[9 + i])
+    left(dsend0, bs_sem.at[9], br_sem.at[9])
+    for base, src0, src1 in ((0, q0s, q1s), (4, g0s, g1s)):
+        left(src0, qs_sem.at[base], qr_sem.at[base])
+        for k in range(1, 4):
+            left(src1, qs_sem.at[base + k], qr_sem.at[base + k])
+    left(ownc.at[0], hs_sem.at[2], hr_sem.at[2])
     for lv in (1, 2):
         left(dsendc.at[0], ss_sem.at[lv], sr_sem.at[lv])
     for i in range(3, 9):
@@ -564,8 +597,13 @@
     left(dkvt, cs_sem.at[3], cr_sem.at[3])
     for i in range(6):
         left(mixs.at[0], ms_sem.at[i], mr_sem.at[i])
-    for part in (part_a, part_b, part_c):
-        stage_left(part)
+    stage_left(part_a)
+    stage_left(part_c)
+    third = stage_end(part_c)
+    second = jnp.concatenate([stage_end(part_b), third], axis=1)
+    gw_ref[:, 1, :] = second[0:12, 0:192]
+    gw_ref[:, 2, :] = pltpu.roll(second, 192, 1)[0:12, 0:192]
+    stage_left(part_b)
 
 
 def deliver(*refs):
@@ -594,16 +632,18 @@
         low(256, 768), low(3, 256, 384), wide(8, 768), wide(3, 8, 384),
         wide(192, 256), wide(192, 128), wide(8, 768), wide(8, 384), low(192, 256), low(192, 256),
         wide(192, 256), wide(3, 192, 128), wide(256, 384),
-        low(2, 256, 384), low(2, 3, 64, 384), low(2, 256, 384), low(2, 128, 384), low(6, 64, 384),
-        low(128, 384), wide(3, 128, 384), wide(2, 3, 2, 64, 384), low(128, 384), low(2, 3, 64, 384),
-        low(2, 128, 384), low(2, 3, 64, 384),
+        low(256, 384), low(2, 3, 64, 384), low(256, 384), low(6, 64, 384),
+        wide(2, 3, 2, 64, 384), low(2, 3, 64, 384), low(2, 3, 64, 384),
+        low(192, 256), low(192, 128), low(192, 256), low(3, 192, 128),
+        low(208, 256), low(208, 128), low(208, 256), low(3, 208, 128),
+        low(256, 768), low(256, 768), low(256, 1152), low(256, 1152),
         low(2, 384, 768), low(384, 768), low(384, 512), low(384, 512), low(384, 256), low(384, 256),
         low(4, 192, 256), low(3, 192, 256), wide(4, 192, 256), low(4, 192, 256), low(3, 192, 256),
         wide(384, 384), low(384, 384), low(64, 384), low(7, 48, 384), low(3, 16, 384),
         wide(384, 256), low(384, 256), low(128, 256), low(3, 96, 256), low(7, 16, 256),
         wide(384, 128), low(384, 128), low(64, 128), low(7, 48, 128), low(3, 16, 128),
         sems(5), sems(11), sems(11), sems(9), sems(9), sems(11), sems(11), sems(3), sems(3),
-        sems(4), sems(4), sems(6), sems(6), sems(9), sems(9), sems(21), sems(21),
+        sems(8), sems(8), sems(4), sems(4), sems(6), sems(6), sems(9), sems(9), sems(21), sems(21),
     ]
     shapes = (
         jax.ShapeDtypeStruct((192, 256), BF16),

time: 49.6 us -> 48.5 us (0.978)
  Pallas kernels: 48.1 us -> 47 us
    pallas_call x1, Pallas kernels: 47.4 us -> 46.3 us  [shards(): pl.pallas_call(kernel, out_shape=shapes, in_specs=[hbm] * 4, out_specs=(v...]
where the time goes in v5:
time: 48.5 us; the launch traced here: 47.7 us
  Pallas kernels  47 us (97%)
  between operations  0.64 us (1%)
    pallas_call x1, Pallas kernels, shards(): pl.pallas_call(kernel, out_shape=shapes, in_specs=[hbm] * 4, out_specs=(v...  46.3 us

profile of v5, /device:TPU:2, one launch (start us, length us, event | category | flops | bytes accessed | tf_op | source)
XLA Modules:
  0.0 47.7 jit_solution(8025508955884786414)
XLA Ops:
  0.6 46.3 %shard_map.75 = (bf16[192,256]{1,0:T(8,128)(2,1)S(1)}, bf16[192,256]{1,0:T(8,128)(2,1)S(1)}, f32[12,3,192]{2,1,0:T(4,128)S(1)}, f32[12,192]{1,0:T(8,128)S(1)}) custom-call(bf16[256,768]{1,0:T(8,128)(2,1)} %bitcast.10, bf16[576,768]{1,0:T(8,128)(2,1)} %bitcast.9, bf16[192,768]{1,0:T(8,128)(2,1)} %wout_hbm.1, bf16[256,768]{1,0:T(8,128)(2,1)} %bitcast.11), custom_call_target="tpu_custom_call" | custom-call | flops 2000000000 | bytes 4000000 | tf_op jit(solution)/shard_map/pallas_call | solution.py:654
  46.9 0.7 %shard_map.76 = (bf16[192,256]{1,0:T(8,128)(2,1)}, bf16[192,256]{1,0:T(8,128)(2,1)}, f32[12,3,192]{2,1,0:T(4,128)}, f32[12,192]{1,0:T(8,128)}) custom-call(bf16[192,256]{1,0:T(8,128)(2,1)S(1)} %get-tuple-element.12.refs_0_, bf16[192,256]{1,0:T(8,128)(2,1)S(1)} %get-tuple-element.13.refs_1_, f32[12,3,192]{2,1,0:T(4,128)S(1)} %get-tuple-element.14.refs_2_, ...), custom_call_target="tpu_custom_call" | custom-call | tf_op jit(solution)/shard_map/pallas_call | solution.py:669

commit v6 on v5

--- a/solution.py
+++ b/solution.py
@@ -434,6 +434,9 @@
         cs_sem.at[2], cr_sem.at[2], {"seq": peer},
     ).start()
 
+    arrived(q0r, qr_sem.at[0], qs_sem.at[0])
+    arrived(g0r, qr_sem.at[4], qs_sem.at[4])
+    down[...] += owner_backward(kv0[1], [(q0r, g0r, far_keep)], qmr0, gmr0, 256)
     att_t = att_s[...]
     for j in range(4):
         mixs[j] = nn(wot[192 * j : 192 * j + 192, :], att_t).astype(BF16)
@@ -442,8 +445,6 @@
             mixs.at[mp_dev(k)], mixr.at[k - 1], ms_sem.at[k - 1], mr_sem.at[k - 1],
             {"mp": mp_dev(k)},
         ).start()
-    for j in range(4):
-        gtacc[j] = nn(wqt[192 * j : 192 * j + 192, :], dq_t)
 
     def widen(blocks):
         at = iota((16 * blocks, 12 * blocks), 0)
@@ -528,9 +529,6 @@
             total = jnp.concatenate([total, jnp.zeros((128 - rows, 384), F32)], axis=0)
         return total.T
 
-    arrived(q0r, qr_sem.at[0], qs_sem.at[0])
-    arrived(g0r, qr_sem.at[4], qs_sem.at[4])
-    down[...] += owner_backward(kv0[1], [(q0r, g0r, far_keep)], qmr0, gmr0, 256)
     total = received(2)
     for lv in (2, 1, 0):
         grad_k = unit_back(uc[lv, 192:384, :], total[0:192]) * 0.5
@@ -552,6 +550,8 @@
     arrived(pdkvt, cr_sem.at[3], cs_sem.at[3])
     stage_one(part_b, own_b + nt(ptg[:, 512:768], pdkvt[0:256, :]))
     stage_one(part_c, own_c + nt(ptg[:, 0:256], pdkvt[256:384, :]))
+    for j in range(4):
+        gtacc[j] = nn(wqt[192 * j : 192 * j + 192, :], dq_t)
     for j in range(4):
         gts[j] = (nn(wkvt[192 * j : 192 * j + 192, :], dkv_t) + gtacc[j]).astype(BF16)
     for k in range(1, 4):

time: 48.5 us -> 48.4 us (level)
  no operation moved by 1% of the time
where the time goes in v6:
time: 48.4 us; the launch traced here: 47.7 us
  Pallas kernels  47 us (97%)
  between operations  0.64 us (1%)
    pallas_call x1, Pallas kernels, shards(): pl.pallas_call(kernel, out_shape=shapes, in_specs=[hbm] * 4, out_specs=(v...  46.3 us

profile of v6, /device:TPU:2, one launch (start us, length us, event | category | flops | bytes accessed | tf_op | source)
XLA Modules:
  0.0 47.7 jit_solution(12466927018092056094)
XLA Ops:
  0.6 46.3 %shard_map.75 = (bf16[192,256]{1,0:T(8,128)(2,1)S(1)}, bf16[192,256]{1,0:T(8,128)(2,1)S(1)}, f32[12,3,192]{2,1,0:T(4,128)S(1)}, f32[12,192]{1,0:T(8,128)S(1)}) custom-call(bf16[256,768]{1,0:T(8,128)(2,1)} %bitcast.10, bf16[576,768]{1,0:T(8,128)(2,1)} %bitcast.9, bf16[192,768]{1,0:T(8,128)(2,1)} %wout_hbm.1, bf16[256,768]{1,0:T(8,128)(2,1)} %bitcast.11), custom_call_target="tpu_custom_call" | custom-call | flops 2000000000 | bytes 4000000 | tf_op jit(solution)/shard_map/pallas_call | solution.py:654
  46.9 0.7 %shard_map.76 = (bf16[192,256]{1,0:T(8,128)(2,1)}, bf16[192,256]{1,0:T(8,128)(2,1)}, f32[12,3,192]{2,1,0:T(4,128)}, f32[12,192]{1,0:T(8,128)}) custom-call(bf16[192,256]{1,0:T(8,128)(2,1)S(1)} %get-tuple-element.12.refs_0_, bf16[192,256]{1,0:T(8,128)(2,1)S(1)} %get-tuple-element.13.refs_1_, f32[12,3,192]{2,1,0:T(4,128)S(1)} %get-tuple-element.14.refs_2_, ...), custom_call_target="tpu_custom_call" | custom-call | tf_op jit(solution)/shard_map/pallas_call | solution.py:669
